TPU v7x, 256 devices: a whole 4x4x8 slice. The times are simulated.
256 devices in a mesh: occ: 8 (over y, x_lo), vir: 32 (over z, x_hi, core).
Axes of the slice: x: 4 (x_hi: 2, x_lo: 2; x = x_hi * 2 + x_lo), y: 4, z: 8, core: 2. Of those that a mesh axis runs over, the one named last changes fastest.
Arguments:
- amplitudes: bfloat16 [2048, 800, 800], P('occ', 'vir'), may hold values from -0.0078125 to 0.0078125
- chol_a: bfloat16 [32, 800, 1600], P(None, 'vir', 'occ'), may hold values from -1 to 1
- chol_b: bfloat16 [4, 800, 1600], P(None, 'vir', 'occ'), may hold values from -1 to 1
Outputs:
- residual: float32 [2048, 128], P('occ', 'vir')
All inputs are finite; a program needn't handle non-finite values.
Results may differ from a plain program's by a relative error of at most 0.0029.
Values may be sent and summed in bfloat16 or wider, within the bound.
No kernel may reach another device: no remote copies, remote signals or barrier semaphores. Data moves between devices by JAX's collectives and lax.ppermute only.
A program may use at most 128 MiB of HBM per device.

v0:
```python
import jax
import jax.numpy as jnp
from jax import lax
from jax.sharding import PartitionSpec as P


def per_device(amplitudes, chol_a, chol_b):
    pair_rows = amplitudes.shape[0]
    local_c = amplitudes.shape[1]
    tile_cols = chol_a.shape[0] * chol_b.shape[0]
    full_a, full_b = (
        lax.all_gather(chol_a, "occ", axis=2, tiled=True),
        lax.all_gather(chol_b, "occ", axis=2, tiled=True),
    )
    piece = lax.all_gather(full_b, "vir", axis=1, tiled=True)
    count = piece.shape[1]
    integrals = jnp.einsum(
        "acp,bdp->cdab", full_a, piece, preferred_element_type=jnp.float32
    ).astype(jnp.bfloat16)
    amps = amplitudes.reshape(pair_rows, local_c * count)
    partial_sum = jnp.dot(
        amps, integrals.reshape(local_c * count, tile_cols), preferred_element_type=jnp.float32
    )
    return lax.psum_scatter(partial_sum, "vir", scatter_dimension=1, tiled=True)


def solution(mesh):
    in_specs = (P("occ", "vir", None), P(None, "vir", "occ"), P(None, "vir", "occ"))
    out_specs = P("occ", "vir")
    return jax.shard_map(
        per_device, mesh=mesh, in_specs=in_specs, out_specs=out_specs, check_vma=False
    )
```

profile of v0, /device:TPU:1, one launch (start us, length us, event | category | flops | bytes accessed | tf_op | source)
XLA Modules:
  0.0 697.8 jit_solution(16124391543988333305)
XLA Ops:
  6.5 0.0 all-gather.5.cloned.1.call-start
  6.5 3.4 copy.9
  10.0 0.0 all-gather.5.cloned.1.call-update
  10.0 0.0 all-gather.3.cloned.1.call-start
  10.0 1.0 copy.7
  11.0 56.1 %all_gather.9 = bf16[4,25,1600]{1,0,2:T(4,128)(2,1)S(1)} all-gather(bf16[4,25,200]{1,0,2:T(4,128)(2,1)S(1)} %copy.7), channel_id=1, replica_groups=mesh['occ'=8,'vir'=32] {'occ'}, dimensions={2}, use_global_device_ids=true | all-gather | bytes 360000 | tf_op jit(solution)/shard_map/all_gather | solution.py:13
  67.2 2.6 copy.8
  69.8 0.0 all-gather.3.cloned.1.call-update
  69.8 0.0 all-reduce.3.cloned.1.call-start
  69.8 223.6 %all-gather.5.cloned.1.call-done = bf16[32,25,1600]{1,0,2:T(8,128)(2,1)} async-done(((bf16[32,25,200]{1,0,2:T(8,128)(2,1)}), bf16[32,25,1600]{1,0,2:T(8,128)(2,1)}) %all-gather.5.cloned.1.call-update) | async-done | bytes 2560016 | tf_op jit(solution)/shard_map/all_gather | solution.py:12
  293.4 14.5 %copy.11 = bf16[32,25,1600]{2,0,1:T(8,128)(2,1)S(1)} copy(bf16[32,25,1600]{1,0,2:T(8,128)(2,1)} %all-gather.5.cloned.1.call-done) | data formatting | bytes 5120000 | tf_op jit(solution)/shard_map/all_gather | solution.py:12
  307.9 101.5 %all-gather.3.cloned.1.call-done = bf16[4,800,1600]{2,0,1:T(4,128)(2,1)} async-done(((bf16[4,25,1600]{2,0,1:T(4,128)(2,1)}), bf16[4,800,1600]{2,0,1:T(4,128)(2,1)}) %all-gather.3.cloned.1.call-update) | async-done | bytes 10240016 | tf_op jit(solution)/shard_map/all_gather | solution.py:15
  409.5 15.4 %convert_bitcast_fusion = bf16[25,800,32,4]{1,2,0,3:T(8,128)(2,1)S(1)} fusion(bf16[4,800,1600,1]{2,0,1,3:T(4,128)(2,1)} %bitcast.15, bf16[32,25,1600]{2,0,1:T(8,128)(2,1)S(1)} %copy.11), kind=kOutput, calls=%fused_computation.2 | convolution fusion | flops 8194560000 | bytes 17920000 | tf_op jit(solution)/shard_map/acp,bdp->cdab/dot_general | solution.py:17
  424.9 5.4 copy.12
  430.3 11.2 %reshape.6 = bf16[20000,128]{0,1:T(8,128)(2,1)} reshape(bf16[25,800,32,4]{1,0,3,2:T(8,128)(2,1)} %copy.12) | data formatting | bytes 10240000 | tf_op jit(solution)/shard_map/reshape | solution.py:22
  441.6 0.0 copy-start
  441.6 7.6 %convolution_bitcast_fusion = f32[256,128]{0,1:T(8,128)} fusion(bf16[20000,128]{0,1:T(8,128)(2,1)} %reshape.6, bf16[256,20000]{0,1:T(8,128)(2,1)} %bitcast.14), kind=kOutput, calls=%fused_computation.4 | convolution fusion | flops 1310720000 | bytes 15491072 | tf_op jit(solution)/shard_map/dot_general | solution.py:21
  449.2 0.0 all-reduce.3.cloned.1.call-update
  449.2 0.0 copy-done
  449.2 0.6 dynamic-slice
  450.5 239.5 %all-reduce.3.cloned.1.call-done = f32[256,128]{0,1:T(8,128)} async-done(((f32[256,128]{0,1:T(8,128)}), f32[256,128]{0,1:T(8,128)}) %all-reduce.3.cloned.1.call-update) | async-done | bytes 131088
  690.0 1.3 constant_dynamic-slice_fusion
Async XLA Ops:
  6.5 286.9 %all-gather.5.cloned.1.call-start = ((), (), s32[]{:S(2)}) async-start(), calls=%async_computation.1 | async-start | bytes 14745600 | tf_op jit(solution)/shard_map/all_gather | solution.py:12
  10.0 399.5 %all-gather.3.cloned.1.call-start = ((), (), s32[]{:S(2)}) async-start(), calls=%async_computation | async-start | bytes 10982400 | tf_op jit(solution)/shard_map/all_gather | solution.py:15
  69.8 620.2 %all-reduce.3.cloned.1.call-start = ((), (), s32[]{:S(2)}) async-start(), calls=%async_computation.2 | async-start | bytes 262144
  441.6 7.7 %copy-start = (u32[256]{0:T(256)S(1)}, u32[256]{0:T(256)}, u32[]{:S(2)}) copy-start(u32[256]{0:T(256)} %constant.5) | copy-start | bytes 3076
Sparse Core Ops, SparseCore 0:
  10.1 283.2 all-gather.4
  296.1 113.3 all-gather.2
  449.3 240.6 all-reduce.2
where the time goes:
time: 698 us
  waiting for transfers between devices  565 us (81%)
  blocking collectives  56.1 us (8%)
  local copies, waits for them, and re-layouts  40.1 us (6%)
  matrix products  23 us (3%)
  between operations  13.8 us (2%)
    unnamed x4, waiting for transfers between devices  240 us
    all_gather x1, waiting for transfers between devices, per_device(): lax.all_gather(chol_a, 'occ', axis=2, tiled=True)  224 us
    all_gather x1, waiting for transfers between devices, per_device(): piece = lax.all_gather(full_b, 'vir', axis=1, tiled=True)  102 us
    all_gather x1, blocking collectives, per_device(): lax.all_gather(chol_b, 'occ', axis=2, tiled=True)  56.1 us
    dot_general x1, matrix products, per_device(): jnp.einsum('acp,bdp->cdab', full_a, piece, preferred_element_type=jnp.flo...  15.4 us
    all_gather x1, local copies, waits for them, and re-layouts, per_device(): lax.all_gather(chol_a, 'occ', axis=2, tiled=True)  14.5 us
  transfers between devices with their start and end apart: 3, of which 3 were waited for; matrix products, arithmetic and copies ran while one was open for 3% of the time, Pallas kernels for 0%

commit v1 on v0

v1 whole, which is shorter than its diff:
```python
import jax
import jax.numpy as jnp
from jax import lax
from jax.experimental import pallas as pl
from jax.experimental.pallas import tpu as pltpu
from jax.sharding import Mesh, PartitionSpec as P

AXES = ("y", "xl", "z", "xh", "c")
SIZES = (4, 2, 8, 2, 2)
NZ = SIZES[2]
PAD = 128
LIMIT = 24 * 1024 * 1024


def spread(t, zd, step=5):
    nc, nv, pairs = t.shape

    def kernel(t_ref, out_ref):
        for z in range(NZ):
            out_ref[z, :, :zd] = t_ref[:, z * zd : (z + 1) * zd]
            out_ref[z, :, zd:] = jnp.zeros((step, PAD - zd, pairs), t.dtype)

    return pl.pallas_call(
        kernel,
        grid=(nc // step,),
        in_specs=[pl.BlockSpec((step, nv, pairs), lambda c: (c, 0, 0))],
        out_specs=pl.BlockSpec((NZ, step, PAD, pairs), lambda c: (0, c, 0, 0)),
        out_shape=jax.ShapeDtypeStruct((2 * NZ, nc, PAD, pairs), t.dtype),
        compiler_params=pltpu.CompilerParams(vmem_limit_bytes=LIMIT),
        cost_estimate=pl.CostEstimate(flops=0, bytes_accessed=30_000_000, transcendentals=0),
    )(t).reshape(2 * NZ, nc * PAD, pairs)


def contract(zs, a, bs, t, acc):
    n = len(zs)
    _, cols, pairs = t.shape
    nc = cols // PAD
    na = a.shape[0] // nc
    nd = bs[0].shape[0] // 2

    def kernel(z_ref, a_ref, *refs):
        b_far, (t_far, acc_ref, out_ref, lhs, b_buf, t_buf, sems) = refs[: 2 * n], refs[2 * n :]

        def copies(k):
            slot = k % 2
            pieces = [(b_far[2 * k + half], b_buf.at[slot, half]) for half in range(2)]
            pieces.append((t_far.at[z_ref[k]], t_buf.at[slot]))
            return [
                pltpu.make_async_copy(src, dst, sems.at[slot, i])
                for i, (src, dst) in enumerate(pieces)
            ]

        for copy in copies(0):
            copy.start()
        lhs[...] = jnp.zeros_like(lhs)
        out_ref[...] = acc_ref[...]
        for k in range(n):
            if k + 1 < n:
                for copy in copies(k + 1):
                    copy.start()
            mine = copies(k)
            for half in range(2):
                mine[half].wait()
            for half in range(2):
                prod = lax.dot_general(
                    a_ref[...], b_buf[k % 2, half], (((1,), (1,)), ((), ())),
                    preferred_element_type=jnp.float32,
                ).astype(jnp.bfloat16)
                for j in range(2):
                    row = (2 * half + j) * na
                    for c in range(nc):
                        lhs[row : row + na, c * PAD : c * PAD + nd] = prod[
                            c * na : (c + 1) * na, j * nd : (j + 1) * nd
                        ]
            mine[2].wait()
            out_ref[...] += jnp.dot(lhs[...], t_buf[k % 2], preferred_element_type=jnp.float32)

    near, far = pl.BlockSpec(memory_space=pltpu.VMEM), pl.BlockSpec(memory_space=pl.ANY)
    return pl.pallas_call(
        kernel,
        grid_spec=pltpu.PrefetchScalarGridSpec(
            num_scalar_prefetch=1,
            grid=(1,),
            in_specs=[near] + [far] * (1 + len(bs)) + [near],
            out_specs=near,
            scratch_shapes=[
                pltpu.VMEM((acc.shape[0], cols), jnp.bfloat16),
                pltpu.VMEM((2, 2) + bs[0].shape, jnp.bfloat16),
                pltpu.VMEM((2,) + t.shape[1:], jnp.bfloat16),
                pltpu.SemaphoreType.DMA((2, 3)),
            ],
        ),
        out_shape=jax.ShapeDtypeStruct(acc.shape, jnp.float32),
        compiler_params=pltpu.CompilerParams(vmem_limit_bytes=40 * 1024 * 1024),
        cost_estimate=pl.CostEstimate(
            flops=n * 2 * 128 * cols * 1600, bytes_accessed=n * 8_000_000, transcendentals=0
        ),
    )(jnp.stack(zs).astype(jnp.int32), a, *bs, t, acc)


def swap(x):
    return lax.ppermute(x, "c", [(0, 1), (1, 0)])


def after(x, *others):
    return lax.optimization_barrier((x,) + others)[0]


def per_device(amplitudes, chol_a, chol_b):
    pairs, nc, nv = amplitudes.shape
    na, _, npl = chol_a.shape
    nb, nd, _ = chol_b.shape
    core, z = lax.axis_index("c"), lax.axis_index("z")
    zd = nv // NZ

    halves = chol_b.reshape(2, nb // 2, nd, npl)
    mine = lax.dynamic_index_in_dim(halves, core, 0, keepdims=False)
    got = swap(lax.dynamic_index_in_dim(halves, 1 - core, 0, keepdims=False))
    both = jnp.where(core == 0, jnp.stack([mine, got]), jnp.stack([got, mine]))
    send = jnp.broadcast_to(both[None], (16,) + both.shape)
    plane = lax.all_to_all(send, ("y", "xl", "xh"), 0, 0)

    amps = spread(amplitudes.transpose(1, 2, 0), zd)
    a_in = chol_a.transpose(1, 0, 2).reshape(nc * na, npl)
    a_send = jnp.broadcast_to(a_in[None], (8,) + a_in.shape)
    plane, amps, a_send = lax.optimization_barrier((plane, amps, a_send))
    plane = plane.reshape(8, 2, 2, nb // 2, nd, npl)
    own = plane.transpose(3, 1, 2, 4, 0, 5).reshape(nb // 2 * zd, 8 * npl)

    away = [(i * 2 + k, (i + 1 - 2 * k) % NZ * 2 + k) for i in range(NZ) for k in range(2)]
    hop = lambda x: lax.ppermute(x, ("z", "c"), away)
    side = 1 - 2 * core
    m1 = hop(own)
    o0 = swap(own)
    o1 = hop(o0)
    a_all = lax.all_to_all(a_send, ("y", "xl"), 0, 0)
    m2, o2 = hop(m1), hop(o1)
    m3, o3 = hop(m2), hop(o2)
    a = a_all.transpose(1, 0, 2).reshape(nc * na, 8 * npl)

    acc = jnp.zeros((nb * na, pairs), jnp.float32)
    at = lambda k: (z - k * side) % NZ
    m3, a = lax.optimization_barrier((m3, a))
    m4 = hop(m3)
    acc = contract(
        [z, at(1), at(-1), at(2), at(-2)], a,
        [own, o0, m1, o1, swap(o1), swap(m1), m2, o2, swap(o2), swap(m2)], amps, acc,
    )
    m4 = after(m4, acc)
    s4 = swap(m4)
    acc = contract([at(3), at(-3)], a, [m3, o3, swap(o3), swap(m3)], amps, acc)
    acc = contract([at(4)], a, [m4, s4], amps, acc)

    res = acc.reshape(2, nb // 2, na, pairs)
    res = jnp.where(core == 0, res, res[::-1]).reshape(nb, na, pairs).transpose(1, 0, 2)
    parts = lax.all_to_all(res, ("z", "xh", "c"), 0, 0)
    return parts.sum(0).T


def solution(mesh):
    fine = Mesh(mesh.devices.reshape(SIZES), AXES)
    occ, vir = ("y", "xl"), ("z", "xh", "c")
    in_specs = (P(occ, vir, None), P(None, vir, occ), P(None, vir, occ))
    return jax.shard_map(
        per_device, mesh=fine, in_specs=in_specs, out_specs=P(occ, vir), check_vma=False
    )
```

time: 698 us -> 129 us (0.18)
  waiting for transfers between devices: 565 us -> 19.4 us
  starting transfers between devices: 0.09 us -> 40.6 us
  blocking collectives: 56.1 us -> 17.7 us
  Pallas kernels: 0 us -> 30.2 us
  matrix products: 23 us -> 0 us
  local copies, waits for them, and re-layouts: 40.1 us -> 19.4 us
  between operations: 13.8 us -> 0.19 us
    all_gather x2 -> x0, waiting for transfers between devices: 325 us -> none  [the longest x1 224 us: per_device(): lax.all_gather(chol_a, 'occ', axis=2, tiled=True)]
    unnamed x4 -> x0, waiting for transfers between devices: 240 us -> none
    all_gather x1 -> x0, blocking collectives: 56.1 us -> none  [per_device(): lax.all_gather(chol_b, 'occ', axis=2, tiled=True)]
    ppermute x0 -> x16, starting transfers between devices: none -> 31.1 us  [the longest x7 23.1 us: per_device(): hop = lambda x: lax.ppermute(x, ('z', 'c'), away)]
    pallas_call x0 -> x4, Pallas kernels: none -> 30.2 us  [the longest x3 25.1 us: contract(): pl.pallas_call(kernel, grid_spec=pltpu.PrefetchScalarGridSpec(num_scalar_...]
    dot_general x2 -> x0, matrix products: 23 us -> none  [the longest x1 15.4 us: per_device(): jnp.einsum('acp,bdp->cdab', full_a, piece, preferred_element_type=jnp.flo...]
    all_to_all x0 -> x1, blocking collectives: none -> 17.7 us  [per_device(): parts = lax.all_to_all(res, ('z', 'xh', 'c'), 0, 0)]
    all_gather x2 -> x0, local copies, waits for them, and re-layouts: 17.1 us -> none  [the longest x1 14.5 us: per_device(): lax.all_gather(chol_a, 'occ', axis=2, tiled=True)]
  transfers between devices with their start and end apart: 3 -> 18, of which waited for: 3 -> 7; matrix products, arithmetic and copies ran while one was open for 3% -> 4% of each run, Pallas kernels for 0% -> 21%
where the time goes in v1:
time: 129 us; the launch traced here: 128 us
  starting transfers between devices  40.6 us (31%)
  Pallas kernels  30.2 us (23%)
  local copies, waits for them, and re-layouts  19.4 us (15%)
  waiting for transfers between devices  19.4 us (15%)
  blocking collectives  17.7 us (14%)
    pallas_call x3, Pallas kernels, contract(): pl.pallas_call(kernel, grid_spec=pltpu.PrefetchScalarGridSpec(num_scalar_...  25.1 us
    ppermute x7, starting transfers between devices, per_device(): hop = lambda x: lax.ppermute(x, ('z', 'c'), away)  23.1 us
    all_to_all x1, blocking collectives, per_device(): parts = lax.all_to_all(res, ('z', 'xh', 'c'), 0, 0)  17.7 us
    ppermute x7, waiting for transfers between devices, per_device(): hop = lambda x: lax.ppermute(x, ('z', 'c'), away)  15.1 us
    unnamed x16, local copies, waits for them, and re-layouts  9.74 us
    ppermute x9, starting transfers between devices, swap(): return lax.ppermute(x, 'c', [(0, 1), (1, 0)])  8.05 us
    pallas_call x1, Pallas kernels, spread(): pl.pallas_call(kernel, grid=(nc // step,), in_specs=[pl.BlockSpec((step,...  5.13 us
    all_to_all x1, starting transfers between devices, per_device(): plane = lax.all_to_all(send, ('y', 'xl', 'xh'), 0, 0)  5.02 us
  transfers between devices with their start and end apart: 18, of which 7 were waited for; matrix products, arithmetic and copies ran while one was open for 4% of the time, Pallas kernels for 21%

profile of v1, /device:TPU:1, one launch (start us, length us, event | category | flops | bytes accessed | tf_op | source)
XLA Modules:
  0.0 128.2 jit_solution(5887799913935057783)
XLA Ops:
  0.9 3.3 %collective-permute-start = (bf16[2,25,200]{2,0,1:T(2,128)(2,1)S(1)}, bf16[2,25,200]{2,0,1:T(2,128)(2,1)S(1)}, u32[]{:S(2)}, u32[]{:S(2)}) collective-permute-start(bf16[2,25,200]{2,0,1:T(2,128)(2,1)S(1)} %get-tuple-element.18), channel_id=1, source_target_pairs={{0,1},{1,0},{2,3},{3,2},{4,5},{5,4},{6,7},{7,6},{8,9},{9,8},{10,11... | collective-permute-start | bytes 60008 | tf_op jit(solution)/shard_map/ppermute | solution.py:102
  4.2 0.9 collective-permute-done
  5.2 1.3 %broadcast_in_dim.16 = bf16[16,2,2,25,200]{4,2,3,1,0:T(2,128)(2,1)} broadcast(bf16[2,2,25,200]{3,1,2,0:T(2,128)(2,1)S(1)} %copy.11), dimensions={1,2,3,4} | broadcast | bytes 680000 | tf_op jit(solution)/shard_map/broadcast_in_dim | solution.py:120
  6.5 5.0 %all-to-all-start = ((bf16[16,2,2,25,200]{4,2,3,1,0:T(2,128)(2,1)}), bf16[16,2,2,25,200]{4,2,3,1,0:T(2,128)(2,1)S(1)}, u32[]{:S(2)}, u32[]{:S(2)}) async-start(bf16[16,2,2,25,200]{4,2,3,1,0:T(2,128)(2,1)} %broadcast_in_dim.16), calls=%async_computation | async-start | bytes 1638400 | tf_op jit(solution)/shard_map/all_to_all | solution.py:121
  11.6 3.9 %copy-done = bf16[256,25,800]{0,2,1:T(8,128)(2,1)S(1)} copy-done((bf16[256,25,800]{0,2,1:T(8,128)(2,1)S(1)}, bf16[256,25,800]{0,2,1:T(8,128)(2,1)}, u32[]{:S(2)}) %copy-start) | copy-done | bytes 10240024
  15.5 5.1 %shard_map.37 = bf16[16,25,128,256]{3,2,1,0:T(8,128)(2,1)} custom-call(bf16[25,800,256]{2,1,0:T(8,128)(2,1)S(1)} %bitcast.32), custom_call_target="tpu_custom_call" | custom-call | bytes 30000000 | tf_op jit(solution)/shard_map/pallas_call | solution.py:23
  20.8 3.5 %all-to-all-done = bf16[16,2,2,25,200]{4,2,3,1,0:T(2,128)(2,1)S(1)} async-done(((bf16[16,2,2,25,200]{4,2,3,1,0:T(2,128)(2,1)}), bf16[16,2,2,25,200]{4,2,3,1,0:T(2,128)(2,1)S(1)}, u32[]{:S(2)}, u32[]{:S(2)}) %all-to-all-start) | async-done | bytes 640032 | tf_op jit(solution)/shard_map/all_to_all | solution.py:121
  24.3 1.8 %broadcast_in_dim.18 = bf16[8,800,200]{1,2,0:T(8,128)(2,1)} broadcast(bf16[800,200]{0,1:T(8,128)(2,1)S(1)} %copy.12), dimensions={1,2} | broadcast | bytes 2880000 | tf_op jit(solution)/shard_map/broadcast_in_dim | solution.py:125
  26.2 0.9 reshape.56.refs_0_
  27.2 1.6 %collective-permute-start.5 = (bf16[200,1600]{1,0:T(8,128)(2,1)S(1)}, bf16[200,1600]{1,0:T(8,128)(2,1)S(1)}, u32[]{:S(2)}, u32[]{:S(2)}) collective-permute-start(bf16[200,1600]{1,0:T(8,128)(2,1)S(1)} %reshape.56.refs_0_), channel_id=1, source_target_pairs={{0,1},{1,0},{2,3},{3,2},{4,5},{5,4},{6,7},{7,6},{8,9},{9,8},{10,11... | collective-permute-start | bytes 1920008 | tf_op jit(solution)/shard_map/ppermute | solution.py:102
  28.8 5.6 %collective-permute-start.1 = (bf16[200,1600]{1,0:T(8,128)(2,1)S(1)}, bf16[200,1600]{1,0:T(8,128)(2,1)S(1)}, u32[]{:S(2)}, u32[]{:S(2)}) collective-permute-start(bf16[200,1600]{1,0:T(8,128)(2,1)S(1)} %reshape.56.refs_0_), channel_id=1, source_target_pairs={{0,4},{1,29},{4,8},{5,1},{8,12},{9,5},{12,16},{13,9},{16,20},{17,1... | collective-permute-start | bytes 1920008 | tf_op jit(solution)/shard_map/ppermute | solution.py:131
  34.4 4.4 %all-to-all-start.1 = ((bf16[8,800,200]{1,2,0:T(8,128)(2,1)}), bf16[8,800,200]{1,2,0:T(8,128)(2,1)}, u32[]{:S(2)}, u32[]{:S(2)}) async-start(bf16[8,800,200]{1,2,0:T(8,128)(2,1)} %broadcast_in_dim.18), calls=%async_computation.1 | async-start | bytes 5734400 | tf_op jit(solution)/shard_map/all_to_all | solution.py:136
  40.5 1.5 %collective-permute-done.1.refs_2_ = bf16[200,1600]{1,0:T(8,128)(2,1)S(1)} collective-permute-done((bf16[200,1600]{1,0:T(8,128)(2,1)S(1)}, bf16[200,1600]{1,0:T(8,128)(2,1)S(1)}, u32[]{:S(2)}, u32[]{:S(2)}) %collective-permute-start.1) | collective-permute-done | bytes 640032 | tf_op jit(solution)/shard_map/ppermute | solution.py:131
  42.0 3.5 %collective-permute-start.2 = (bf16[200,1600]{1,0:T(8,128)(2,1)S(1)}, bf16[200,1600]{1,0:T(8,128)(2,1)}, u32[]{:S(2)}, u32[]{:S(2)}) collective-permute-start(bf16[200,1600]{1,0:T(8,128)(2,1)S(1)} %collective-permute-done.1.refs_2_), channel_id=1, source_target_pairs={{0,4},{1,29},{4,8},{5,1},{8,12},{9,5},{12,16},{13,9},{16,20},{17,1... | collective-permute-start | bytes 1920008 | tf_op jit(solution)/shard_map/ppermute | solution.py:131
  45.5 3.6 %collective-permute-done.6.refs_3_ = bf16[200,1600]{1,0:T(8,128)(2,1)} collective-permute-done((bf16[200,1600]{1,0:T(8,128)(2,1)S(1)}, bf16[200,1600]{1,0:T(8,128)(2,1)}, u32[]{:S(2)}, u32[]{:S(2)}) %collective-permute-start.6) | collective-permute-done | bytes 640032 | tf_op jit(solution)/shard_map/ppermute | solution.py:131
  49.1 3.5 %collective-permute-start.9 = (bf16[200,1600]{1,0:T(8,128)(2,1)}, bf16[200,1600]{1,0:T(8,128)(2,1)}, u32[]{:S(2)}, u32[]{:S(2)}) collective-permute-start(bf16[200,1600]{1,0:T(8,128)(2,1)} %collective-permute-done.6.refs_3_), channel_id=1, source_target_pairs={{0,4},{1,29},{4,8},{5,1},{8,12},{9,5},{12,16},{13,9},{16,20},{17,1... | collective-permute-start | bytes 1920008 | tf_op jit(solution)/shard_map/ppermute | solution.py:131
  52.6 3.6 %collective-permute-done.2.refs_6_ = bf16[200,1600]{1,0:T(8,128)(2,1)} collective-permute-done((bf16[200,1600]{1,0:T(8,128)(2,1)S(1)}, bf16[200,1600]{1,0:T(8,128)(2,1)}, u32[]{:S(2)}, u32[]{:S(2)}) %collective-permute-start.2) | collective-permute-done | bytes 640032 | tf_op jit(solution)/shard_map/ppermute | solution.py:131
  56.3 3.5 %collective-permute-start.3 = (bf16[200,1600]{1,0:T(8,128)(2,1)}, bf16[200,1600]{1,0:T(8,128)(2,1)}, u32[]{:S(2)}, u32[]{:S(2)}) collective-permute-start(bf16[200,1600]{1,0:T(8,128)(2,1)} %collective-permute-done.2.refs_6_), channel_id=1, source_target_pairs={{0,4},{1,29},{4,8},{5,1},{8,12},{9,5},{12,16},{13,9},{16,20},{17,1... | collective-permute-start | bytes 1920008 | tf_op jit(solution)/shard_map/ppermute | solution.py:131
  59.8 0.9 copy-done.3
  61.2 2.3 %collective-permute-done.9.refs_7_ = bf16[200,1600]{1,0:T(8,128)(2,1)} collective-permute-done((bf16[200,1600]{1,0:T(8,128)(2,1)}, bf16[200,1600]{1,0:T(8,128)(2,1)}, u32[]{:S(2)}, u32[]{:S(2)}) %collective-permute-start.9) | collective-permute-done | bytes 640032 | tf_op jit(solution)/shard_map/ppermute | solution.py:131
  63.5 3.2 %collective-permute-start.13 = (bf16[200,1600]{1,0:T(8,128)(2,1)}, bf16[200,1600]{1,0:T(8,128)(2,1)}, u32[]{:S(2)}, u32[]{:S(2)}) collective-permute-start(bf16[200,1600]{1,0:T(8,128)(2,1)} %collective-permute-done.9.refs_7_), channel_id=1, source_target_pairs={{0,4},{1,29},{4,8},{5,1},{8,12},{9,5},{12,16},{13,9},{16,20},{17,1... | collective-permute-start | bytes 1920008 | tf_op jit(solution)/shard_map/ppermute | solution.py:131
  66.7 4.0 %collective-permute-done.3.refs_0_ = bf16[200,1600]{1,0:T(8,128)(2,1)} collective-permute-done((bf16[200,1600]{1,0:T(8,128)(2,1)}, bf16[200,1600]{1,0:T(8,128)(2,1)}, u32[]{:S(2)}, u32[]{:S(2)}) %collective-permute-start.3) | collective-permute-done | bytes 640032 | tf_op jit(solution)/shard_map/ppermute | solution.py:131
  70.6 1.4 %collective-permute-start.10 = (bf16[200,1600]{1,0:T(8,128)(2,1)}, bf16[200,1600]{1,0:T(8,128)(2,1)}, u32[]{:S(2)}, u32[]{:S(2)}) collective-permute-start(bf16[200,1600]{1,0:T(8,128)(2,1)} %collective-permute-done.9.refs_7_), channel_id=1, source_target_pairs={{0,1},{1,0},{2,3},{3,2},{4,5},{5,4},{6,7},{7,6},{8,9},{9,8},{10,11... | collective-permute-start | bytes 1920008 | tf_op jit(solution)/shard_map/ppermute | solution.py:102
  72.9 3.0 %collective-permute-start.4 = (bf16[200,1600]{1,0:T(8,128)(2,1)}, bf16[200,1600]{1,0:T(8,128)(2,1)}, u32[]{:S(2)}, u32[]{:S(2)}) collective-permute-start(bf16[200,1600]{1,0:T(8,128)(2,1)} %collective-permute-done.3.refs_0_), channel_id=1, source_target_pairs={{0,4},{1,29},{4,8},{5,1},{8,12},{9,5},{12,16},{13,9},{16,20},{17,1... | collective-permute-start | bytes 1920008 | tf_op jit(solution)/shard_map/ppermute | solution.py:131
  75.9 4.1 %copy.16.a_ref = bf16[800,1600]{1,0:T(8,128)(2,1)S(1)} copy(bf16[800,1600]{0,1:T(8,128)(2,1)} %bitcast.10) | data formatting | bytes 5120000 | tf_op jit(solution)/shard_map/optimization_barrier | solution.py:143
  80.9 1.1 copy-done.2
  82.0 1.1 copy-done.4
  83.1 1.1 copy-done.6
  84.2 14.5 %shard_map.38.refs_5_ = f32[128,256]{1,0:T(8,128)S(1)} custom-call(s32[5]{0:T(128)S(1)} %stack.51.z_ref, bf16[800,1600]{1,0:T(8,128)(2,1)S(1)} %copy.16.a_ref, bf16[200,1600]{1,0:T(8,128)(2,1)S(1)} %reshape.56.refs_0_, bf16[200,1600]{1,0:T(8,128)(2,1)S(1)} %copy-done.2, bf16[200,1600]{1,0:T(8,128)(2,1)S(1)} %copy-done.4, ...), custom_call_target="tpu_custom_call" | custom-call | flops 6553600000 | bytes 40000000 | tf_op jit(solution)/shard_map/pallas_call | solution.py:79
  99.2 6.9 %shard_map.39.refs_3_ = f32[128,256]{1,0:T(8,128)S(1)} custom-call(s32[2]{0:T(128)S(1)} %pad_add_fusion.z_ref, bf16[800,1600]{1,0:T(8,128)(2,1)S(1)} %copy.16.a_ref, bf16[200,1600]{1,0:T(8,128)(2,1)} %collective-permute-done.3.refs_0_, bf16[200,1600]{1,0:T(8,128)(2,1)} %collective-permute-done.13.refs_1_, bf16[200,1600]{1,0:T(8,128)(2,1)} %collective-permute-done.14.refs_2_, ...), custom_call_target="tpu_custom_call" | custom-call | flops 2621440000 | bytes 16000000 | tf_op jit(solution)/shard_map/pallas_call | solution.py:79
  106.1 3.7 %shard_map.40 = f32[128,256]{1,0:T(8,128)S(1)} custom-call(s32[1]{0:T(128)} %bitcast.z_ref, bf16[800,1600]{1,0:T(8,128)(2,1)S(1)} %copy.16.a_ref, bf16[200,1600]{1,0:T(8,128)(2,1)} %collective-permute-done.4.refs_0_, bf16[200,1600]{1,0:T(8,128)(2,1)S(1)} %collective-permute-done.12.refs_1_, bf16[16,3200,256]{2,1,0:T(8,128)(2,1)} %bitcast.36, ...), custom_call_target="tpu_custom_call" | custom-call | flops 1310720000 | bytes 8000000 | tf_op jit(solution)/shard_map/pallas_call | solution.py:79
  109.9 17.7 %all_to_all.15 = f32[32,4,256]{2,1,0:T(4,128)S(1)} all-to-all(f32[32,4,256]{2,1,0:T(4,128)S(1)} %bitcast.39), channel_id=1, replica_groups=mesh['y'=4,'xl'=2,'z'=8,'xh'=2,'c'=2] {'z','xh','c'}, dimensions={0} | all-to-all | bytes 262144 | tf_op jit(solution)/shard_map/all_to_all | solution.py:156
  (41 shorter events, 6.5 us)
Async XLA Ops:
  0.9 4.2 %collective-permute-start = (bf16[2,25,200]{2,0,1:T(2,128)(2,1)S(1)}, bf16[2,25,200]{2,0,1:T(2,128)(2,1)S(1)}, u32[]{:S(2)}, u32[]{:S(2)}) collective-permute-start(bf16[2,25,200]{2,0,1:T(2,128)(2,1)S(1)} %get-tuple-element.18), channel_id=1, source_target_pairs={{0,1},{1,0},{2,3},{3,2},{4,5},{5,4},{6,7},{7,6},{8,9},{9,8},{10,11... | collective-permute-start | bytes 60008 | tf_op jit(solution)/shard_map/ppermute | solution.py:102
  6.5 17.8 %all-to-all-start = ((bf16[16,2,2,25,200]{4,2,3,1,0:T(2,128)(2,1)}), bf16[16,2,2,25,200]{4,2,3,1,0:T(2,128)(2,1)S(1)}, u32[]{:S(2)}, u32[]{:S(2)}) async-start(bf16[16,2,2,25,200]{4,2,3,1,0:T(2,128)(2,1)} %broadcast_in_dim.16), calls=%async_computation | async-start | bytes 1638400 | tf_op jit(solution)/shard_map/all_to_all | solution.py:121
  11.6 3.9 %copy-start = (bf16[256,25,800]{0,2,1:T(8,128)(2,1)S(1)}, bf16[256,25,800]{0,2,1:T(8,128)(2,1)}, u32[]{:S(2)}) copy-start(bf16[256,25,800]{0,2,1:T(8,128)(2,1)} %param.3) | copy-start | bytes 30720004
  15.5 5.1 %copy-start.7 = (bf16[32,25,200]{2,0,1:T(8,128)(2,1)S(1)}, bf16[32,25,200]{2,0,1:T(8,128)(2,1)}, u32[]{:S(2)}) copy-start(bf16[32,25,200]{2,0,1:T(8,128)(2,1)} %param.4) | copy-start | bytes 960004
  27.2 11.6 %collective-permute-start.5 = (bf16[200,1600]{1,0:T(8,128)(2,1)S(1)}, bf16[200,1600]{1,0:T(8,128)(2,1)S(1)}, u32[]{:S(2)}, u32[]{:S(2)}) collective-permute-start(bf16[200,1600]{1,0:T(8,128)(2,1)S(1)} %reshape.56.refs_0_), channel_id=1, source_target_pairs={{0,1},{1,0},{2,3},{3,2},{4,5},{5,4},{6,7},{7,6},{8,9},{9,8},{10,11... | collective-permute-start | bytes 1920008 | tf_op jit(solution)/shard_map/ppermute | solution.py:102
  28.8 13.2 %collective-permute-start.1 = (bf16[200,1600]{1,0:T(8,128)(2,1)S(1)}, bf16[200,1600]{1,0:T(8,128)(2,1)S(1)}, u32[]{:S(2)}, u32[]{:S(2)}) collective-permute-start(bf16[200,1600]{1,0:T(8,128)(2,1)S(1)} %reshape.56.refs_0_), channel_id=1, source_target_pairs={{0,4},{1,29},{4,8},{5,1},{8,12},{9,5},{12,16},{13,9},{16,20},{17,1... | collective-permute-start | bytes 1920008 | tf_op jit(solution)/shard_map/ppermute | solution.py:131
  34.4 37.7 %all-to-all-start.1 = ((bf16[8,800,200]{1,2,0:T(8,128)(2,1)}), bf16[8,800,200]{1,2,0:T(8,128)(2,1)}, u32[]{:S(2)}, u32[]{:S(2)}) async-start(bf16[8,800,200]{1,2,0:T(8,128)(2,1)} %broadcast_in_dim.18), calls=%async_computation.1 | async-start | bytes 5734400 | tf_op jit(solution)/shard_map/all_to_all | solution.py:136
  38.8 10.3 %collective-permute-start.6 = (bf16[200,1600]{1,0:T(8,128)(2,1)S(1)}, bf16[200,1600]{1,0:T(8,128)(2,1)}, u32[]{:S(2)}, u32[]{:S(2)}) collective-permute-start(bf16[200,1600]{1,0:T(8,128)(2,1)S(1)} %collective-permute-done.5.refs_1_), channel_id=1, source_target_pairs={{0,4},{1,29},{4,8},{5,1},{8,12},{9,5},{12,16},{13,9},{16,20},{17,1... | collective-permute-start | bytes 1920008 | tf_op jit(solution)/shard_map/ppermute | solution.py:131
  39.6 0.9 copy-start.1
  42.0 14.3 %collective-permute-start.2 = (bf16[200,1600]{1,0:T(8,128)(2,1)S(1)}, bf16[200,1600]{1,0:T(8,128)(2,1)}, u32[]{:S(2)}, u32[]{:S(2)}) collective-permute-start(bf16[200,1600]{1,0:T(8,128)(2,1)S(1)} %collective-permute-done.1.refs_2_), channel_id=1, source_target_pairs={{0,4},{1,29},{4,8},{5,1},{8,12},{9,5},{12,16},{13,9},{16,20},{17,1... | collective-permute-start | bytes 1920008 | tf_op jit(solution)/shard_map/ppermute | solution.py:131
  49.1 14.4 %collective-permute-start.9 = (bf16[200,1600]{1,0:T(8,128)(2,1)}, bf16[200,1600]{1,0:T(8,128)(2,1)}, u32[]{:S(2)}, u32[]{:S(2)}) collective-permute-start(bf16[200,1600]{1,0:T(8,128)(2,1)} %collective-permute-done.6.refs_3_), channel_id=1, source_target_pairs={{0,4},{1,29},{4,8},{5,1},{8,12},{9,5},{12,16},{13,9},{16,20},{17,1... | collective-permute-start | bytes 1920008 | tf_op jit(solution)/shard_map/ppermute | solution.py:131
  56.3 14.4 %collective-permute-start.3 = (bf16[200,1600]{1,0:T(8,128)(2,1)}, bf16[200,1600]{1,0:T(8,128)(2,1)}, u32[]{:S(2)}, u32[]{:S(2)}) collective-permute-start(bf16[200,1600]{1,0:T(8,128)(2,1)} %collective-permute-done.2.refs_6_), channel_id=1, source_target_pairs={{0,4},{1,29},{4,8},{5,1},{8,12},{9,5},{12,16},{13,9},{16,20},{17,1... | collective-permute-start | bytes 1920008 | tf_op jit(solution)/shard_map/ppermute | solution.py:131
  59.8 12.3 %collective-permute-start.8 = (bf16[200,1600]{1,0:T(8,128)(2,1)S(1)}, bf16[200,1600]{1,0:T(8,128)(2,1)S(1)}, u32[]{:S(2)}, u32[]{:S(2)}) collective-permute-start(bf16[200,1600]{1,0:T(8,128)(2,1)S(1)} %collective-permute-done.1.refs_2_), channel_id=1, source_target_pairs={{0,1},{1,0},{2,3},{3,2},{4,5},{5,4},{6,7},{7,6},{8,9},{9,8},{10,11... | collective-permute-start | bytes 1920008 | tf_op jit(solution)/shard_map/ppermute | solution.py:102
  59.8 0.9 copy-start.3
  60.7 19.4 %collective-permute-start.11 = (bf16[200,1600]{1,0:T(8,128)(2,1)}, bf16[200,1600]{1,0:T(8,128)(2,1)}, u32[]{:S(2)}, u32[]{:S(2)}) collective-permute-start(bf16[200,1600]{1,0:T(8,128)(2,1)} %collective-permute-done.2.refs_6_), channel_id=1, source_target_pairs={{0,1},{1,0},{2,3},{3,2},{4,5},{5,4},{6,7},{7,6},{8,9},{9,8},{10,11... | collective-permute-start | bytes 1920008 | tf_op jit(solution)/shard_map/ppermute | solution.py:102
  63.5 16.9 %collective-permute-start.13 = (bf16[200,1600]{1,0:T(8,128)(2,1)}, bf16[200,1600]{1,0:T(8,128)(2,1)}, u32[]{:S(2)}, u32[]{:S(2)}) collective-permute-start(bf16[200,1600]{1,0:T(8,128)(2,1)} %collective-permute-done.9.refs_7_), channel_id=1, source_target_pairs={{0,4},{1,29},{4,8},{5,1},{8,12},{9,5},{12,16},{13,9},{16,20},{17,1... | collective-permute-start | bytes 1920008 | tf_op jit(solution)/shard_map/ppermute | solution.py:131
  66.7 14.2 %collective-permute-start.7 = (bf16[200,1600]{1,0:T(8,128)(2,1)}, bf16[200,1600]{1,0:T(8,128)(2,1)}, u32[]{:S(2)}, u32[]{:S(2)}) collective-permute-start(bf16[200,1600]{1,0:T(8,128)(2,1)} %collective-permute-done.6.refs_3_), channel_id=1, source_target_pairs={{0,1},{1,0},{2,3},{3,2},{4,5},{5,4},{6,7},{7,6},{8,9},{9,8},{10,11... | collective-permute-start | bytes 1920008 | tf_op jit(solution)/shard_map/ppermute | solution.py:102
  70.6 10.2 %collective-permute-start.10 = (bf16[200,1600]{1,0:T(8,128)(2,1)}, bf16[200,1600]{1,0:T(8,128)(2,1)}, u32[]{:S(2)}, u32[]{:S(2)}) collective-permute-start(bf16[200,1600]{1,0:T(8,128)(2,1)} %collective-permute-done.9.refs_7_), channel_id=1, source_target_pairs={{0,1},{1,0},{2,3},{3,2},{4,5},{5,4},{6,7},{7,6},{8,9},{9,8},{10,11... | collective-permute-start | bytes 1920008 | tf_op jit(solution)/shard_map/ppermute | solution.py:102
  72.0 0.8 copy-start.5
  72.9 25.8 %collective-permute-start.4 = (bf16[200,1600]{1,0:T(8,128)(2,1)}, bf16[200,1600]{1,0:T(8,128)(2,1)}, u32[]{:S(2)}, u32[]{:S(2)}) collective-permute-start(bf16[200,1600]{1,0:T(8,128)(2,1)} %collective-permute-done.3.refs_0_), channel_id=1, source_target_pairs={{0,4},{1,29},{4,8},{5,1},{8,12},{9,5},{12,16},{13,9},{16,20},{17,1... | collective-permute-start | bytes 1920008 | tf_op jit(solution)/shard_map/ppermute | solution.py:131
  80.1 19.1 %collective-permute-start.15 = (bf16[200,1600]{1,0:T(8,128)(2,1)}, bf16[200,1600]{1,0:T(8,128)(2,1)}, u32[]{:S(2)}, u32[]{:S(2)}) collective-permute-start(bf16[200,1600]{1,0:T(8,128)(2,1)} %collective-permute-done.3.refs_0_), channel_id=1, source_target_pairs={{0,1},{1,0},{2,3},{3,2},{4,5},{5,4},{6,7},{7,6},{8,9},{9,8},{10,11... | collective-permute-start | bytes 1920008 | tf_op jit(solution)/shard_map/ppermute | solution.py:102
  80.4 18.8 %collective-permute-start.14 = (bf16[200,1600]{1,0:T(8,128)(2,1)}, bf16[200,1600]{1,0:T(8,128)(2,1)}, u32[]{:S(2)}, u32[]{:S(2)}) collective-permute-start(bf16[200,1600]{1,0:T(8,128)(2,1)} %collective-permute-done.13.refs_1_), channel_id=1, source_target_pairs={{0,1},{1,0},{2,3},{3,2},{4,5},{5,4},{6,7},{7,6},{8,9},{9,8},{10,11... | collective-permute-start | bytes 1920008 | tf_op jit(solution)/shard_map/ppermute | solution.py:102
  80.9 1.1 copy-start.2
  82.0 1.1 copy-start.4
  83.1 1.1 copy-start.6
  98.7 7.4 %collective-permute-start.12 = (bf16[200,1600]{1,0:T(8,128)(2,1)}, bf16[200,1600]{1,0:T(8,128)(2,1)S(1)}, u32[]{:S(2)}, u32[]{:S(2)}) collective-permute-start(bf16[200,1600]{1,0:T(8,128)(2,1)} %collective-permute-done.4.refs_0_), channel_id=1, source_target_pairs={{0,1},{1,0},{2,3},{3,2},{4,5},{5,4},{6,7},{7,6},{8,9},{9,8},{10,11... | collective-permute-start | bytes 1920008 | tf_op jit(solution)/shard_map/ppermute | solution.py:102

commit v2 on v1

--- a/solution.py
+++ b/solution.py
@@ -25,10 +25,10 @@
         grid=(nc // step,),
         in_specs=[pl.BlockSpec((step, nv, pairs), lambda c: (c, 0, 0))],
         out_specs=pl.BlockSpec((NZ, step, PAD, pairs), lambda c: (0, c, 0, 0)),
-        out_shape=jax.ShapeDtypeStruct((2 * NZ, nc, PAD, pairs), t.dtype),
+        out_shape=jax.ShapeDtypeStruct((NZ, nc, PAD, pairs), t.dtype),
         compiler_params=pltpu.CompilerParams(vmem_limit_bytes=LIMIT),
         cost_estimate=pl.CostEstimate(flops=0, bytes_accessed=30_000_000, transcendentals=0),
-    )(t).reshape(2 * NZ, nc * PAD, pairs)
+    )(t).reshape(NZ, nc * PAD, pairs)
 
 
 def contract(zs, a, bs, t, acc):
@@ -55,12 +55,12 @@
         lhs[...] = jnp.zeros_like(lhs)
         out_ref[...] = acc_ref[...]
         for k in range(n):
+            mine = copies(k)
+            for half in range(2):
+                mine[half].wait()
             if k + 1 < n:
                 for copy in copies(k + 1):
                     copy.start()
-            mine = copies(k)
-            for half in range(2):
-                mine[half].wait()
             for half in range(2):
                 prod = lax.dot_general(
                     a_ref[...], b_buf[k % 2, half], (((1,), (1,)), ((), ())),
@@ -75,6 +75,8 @@
             mine[2].wait()
             out_ref[...] += jnp.dot(lhs[...], t_buf[k % 2], preferred_element_type=jnp.float32)
 
+    t, *bs = (pltpu.with_memory_space_constraint(x, pltpu.HBM) for x in (t, *bs))
+    a = pltpu.with_memory_space_constraint(a, pltpu.VMEM)
     near, far = pl.BlockSpec(memory_space=pltpu.VMEM), pl.BlockSpec(memory_space=pl.ANY)
     return pl.pallas_call(
         kernel,
@@ -114,11 +116,9 @@
     zd = nv // NZ
 
     halves = chol_b.reshape(2, nb // 2, nd, npl)
-    mine = lax.dynamic_index_in_dim(halves, core, 0, keepdims=False)
-    got = swap(lax.dynamic_index_in_dim(halves, 1 - core, 0, keepdims=False))
-    both = jnp.where(core == 0, jnp.stack([mine, got]), jnp.stack([got, mine]))
-    send = jnp.broadcast_to(both[None], (16,) + both.shape)
-    plane = lax.all_to_all(send, ("y", "xl", "xh"), 0, 0)
+    send = jnp.broadcast_to(halves[None], (16,) + halves.shape)
+    send = send.reshape((32,) + halves.shape[1:])
+    plane = lax.all_to_all(send, ("y", "xl", "xh", "c"), 0, 0)
 
     amps = spread(amplitudes.transpose(1, 2, 0), zd)
     a_in = chol_a.transpose(1, 0, 2).reshape(nc * na, npl)

time: 129 us -> 124 us (0.961)
  starting transfers between devices: 40.6 us -> 37.3 us
  Pallas kernels: 30.2 us -> 27.5 us
  waiting for transfers between devices: 19.4 us -> 22 us
    ppermute x9 -> x8, starting transfers between devices: 8.05 us -> 3.48 us  [swap(): return lax.ppermute(x, 'c', [(0, 1), (1, 0)])]
    all_to_all x1, starting transfers between devices: 5.02 us -> 8.59 us  [per_device(): plane = lax.all_to_all(send, ('y', 'xl', 'xh', 'c'), 0, 0)]
    pallas_call x1, Pallas kernels: 5.13 us -> 1.92 us  [spread(): pl.pallas_call(kernel, grid=(nc // step,), in_specs=[pl.BlockSpec((step,...]
    ppermute x7, waiting for transfers between devices: 15.1 us -> 18.2 us  [per_device(): hop = lambda x: lax.ppermute(x, ('z', 'c'), away)]
    ppermute x7, starting transfers between devices: 23.1 us -> 21.6 us  [per_device(): hop = lambda x: lax.ppermute(x, ('z', 'c'), away)]
    unnamed x16 -> x12, local copies, waits for them, and re-layouts: 9.74 us -> 8.63 us
  transfers between devices with their start and end apart: 18 -> 17, of which waited for: 7 -> 6; matrix products, arithmetic and copies ran while one was open for 4% -> 4% of each run, Pallas kernels for 21% -> 19%
where the time goes in v2:
time: 124 us
  starting transfers between devices  37.3 us (30%)
  Pallas kernels  27.5 us (22%)
  waiting for transfers between devices  22 us (18%)
  local copies, waits for them, and re-layouts  18.2 us (15%)
  blocking collectives  17.8 us (14%)
    pallas_call x3, Pallas kernels, contract(): pl.pallas_call(kernel, grid_spec=pltpu.PrefetchScalarGridSpec(num_scalar_...  25.6 us
    ppermute x7, starting transfers between devices, per_device(): hop = lambda x: lax.ppermute(x, ('z', 'c'), away)  21.6 us
    ppermute x7, waiting for transfers between devices, per_device(): hop = lambda x: lax.ppermute(x, ('z', 'c'), away)  18.2 us
    all_to_all x1, blocking collectives, per_device(): parts = lax.all_to_all(res, ('z', 'xh', 'c'), 0, 0)  17.8 us
    unnamed x12, local copies, waits for them, and re-layouts  8.63 us
    all_to_all x1, starting transfers between devices, per_device(): plane = lax.all_to_all(send, ('y', 'xl', 'xh', 'c'), 0, 0)  8.59 us
    optimization_barrier x1, local copies, waits for them, and re-layouts, per_device(): m3, a = lax.optimization_barrier((m3, a))  4.13 us
    all_to_all x1, waiting for transfers between devices, per_device(): plane = lax.all_to_all(send, ('y', 'xl', 'xh', 'c'), 0, 0)  3.83 us
  transfers between devices with their start and end apart: 17, of which 6 were waited for; matrix products, arithmetic and copies ran while one was open for 4% of the time, Pallas kernels for 19%

profile of v2, /device:TPU:1, one launch (start us, length us, event | category | flops | bytes accessed | tf_op | source)
XLA Modules:
  0.0 123.9 jit_solution(12579424815064172482)
XLA Ops:
  0.0 0.8 broadcast_in_dim.17
  0.9 1.3 %broadcast_in_dim.18 = bf16[16,2,2,25,200]{4,2,3,1,0:T(2,128)(2,1)} broadcast(bf16[2,2,25,200]{3,1,2,0:T(2,128)(2,1)S(1)} %copy.11), dimensions={1,2,3,4} | broadcast | bytes 680000 | tf_op jit(solution)/shard_map/broadcast_in_dim | solution.py:119
  2.2 8.6 %all-to-all-start = ((bf16[32,2,25,200]{3,1,2,0:T(2,128)(2,1)}), bf16[32,2,25,200]{3,1,2,0:T(2,128)(2,1)S(1)}, u32[]{:S(2)}, u32[]{:S(2)}) async-start(bf16[32,2,25,200]{3,1,2,0:T(2,128)(2,1)} %bitcast.1), calls=%async_computation | async-start | bytes 1638400 | tf_op jit(solution)/shard_map/all_to_all | solution.py:121
  10.8 3.9 %copy-done.1 = bf16[256,25,800]{0,2,1:T(8,128)(2,1)S(1)} copy-done((bf16[256,25,800]{0,2,1:T(8,128)(2,1)S(1)}, bf16[256,25,800]{0,2,1:T(8,128)(2,1)}, u32[]{:S(2)}) %copy-start.1) | copy-done | bytes 10240024
  14.7 1.9 %shard_map.37 = bf16[8,25,128,256]{3,2,1,0:T(8,128)(2,1)S(1)} custom-call(bf16[25,800,256]{2,1,0:T(8,128)(2,1)S(1)} %bitcast.33), custom_call_target="tpu_custom_call" | custom-call | bytes 30000000 | tf_op jit(solution)/shard_map/pallas_call | solution.py:23
  16.7 4.7 %copy-done = bf16[8,25,128,256]{3,2,1,0:T(8,128)(2,1)} copy-done((bf16[8,25,128,256]{3,2,1,0:T(8,128)(2,1)}, bf16[8,25,128,256]{3,2,1,0:T(8,128)(2,1)S(1)}, u32[]{:S(2)}) %copy-start) | copy-done | bytes 13107224
  21.6 3.8 %all-to-all-done = bf16[32,2,25,200]{3,1,2,0:T(2,128)(2,1)S(1)} async-done(((bf16[32,2,25,200]{3,1,2,0:T(2,128)(2,1)}), bf16[32,2,25,200]{3,1,2,0:T(2,128)(2,1)S(1)}, u32[]{:S(2)}, u32[]{:S(2)}) %all-to-all-start) | async-done | bytes 640032 | tf_op jit(solution)/shard_map/all_to_all | solution.py:121
  25.4 1.8 %broadcast_in_dim.20 = bf16[8,800,200]{1,2,0:T(8,128)(2,1)} broadcast(bf16[800,200]{0,1:T(8,128)(2,1)S(1)} %copy.12), dimensions={1,2} | broadcast | bytes 2880000 | tf_op jit(solution)/shard_map/broadcast_in_dim | solution.py:125
  27.4 0.9 reshape.26.refs_0_
  28.4 5.7 %collective-permute-start = (bf16[200,1600]{1,0:T(8,128)(2,1)S(1)}, bf16[200,1600]{1,0:T(8,128)(2,1)}, u32[]{:S(2)}, u32[]{:S(2)}) collective-permute-start(bf16[200,1600]{1,0:T(8,128)(2,1)S(1)} %reshape.26.refs_0_), channel_id=1, source_target_pairs={{0,4},{1,29},{4,8},{5,1},{8,12},{9,5},{12,16},{13,9},{16,20},{17,1... | collective-permute-start | bytes 1920008 | tf_op jit(solution)/shard_map/ppermute | solution.py:131
  34.0 3.6 %all-to-all-start.1 = ((bf16[8,800,200]{1,2,0:T(8,128)(2,1)}), bf16[8,800,200]{1,2,0:T(8,128)(2,1)S(1)}, u32[]{:S(2)}, u32[]{:S(2)}) async-start(bf16[8,800,200]{1,2,0:T(8,128)(2,1)} %broadcast_in_dim.20), calls=%async_computation.1 | async-start | bytes 5734400 | tf_op jit(solution)/shard_map/all_to_all | solution.py:136
  37.7 0.8 collective-permute-start.5
  38.5 3.2 %collective-permute-done.refs_2_ = bf16[200,1600]{1,0:T(8,128)(2,1)} collective-permute-done((bf16[200,1600]{1,0:T(8,128)(2,1)S(1)}, bf16[200,1600]{1,0:T(8,128)(2,1)}, u32[]{:S(2)}, u32[]{:S(2)}) %collective-permute-start) | collective-permute-done | bytes 640032 | tf_op jit(solution)/shard_map/ppermute | solution.py:131
  41.7 3.4 %collective-permute-start.1 = (bf16[200,1600]{1,0:T(8,128)(2,1)}, bf16[200,1600]{1,0:T(8,128)(2,1)}, u32[]{:S(2)}, u32[]{:S(2)}) collective-permute-start(bf16[200,1600]{1,0:T(8,128)(2,1)} %collective-permute-done.refs_2_), channel_id=1, source_target_pairs={{0,4},{1,29},{4,8},{5,1},{8,12},{9,5},{12,16},{13,9},{16,20},{17,1... | collective-permute-start | bytes 1920008 | tf_op jit(solution)/shard_map/ppermute | solution.py:131
  45.1 3.8 %collective-permute-done.5.refs_3_ = bf16[200,1600]{1,0:T(8,128)(2,1)} collective-permute-done((bf16[200,1600]{1,0:T(8,128)(2,1)}, bf16[200,1600]{1,0:T(8,128)(2,1)}, u32[]{:S(2)}, u32[]{:S(2)}) %collective-permute-start.5) | collective-permute-done | bytes 640032 | tf_op jit(solution)/shard_map/ppermute | solution.py:131
  48.9 3.3 %collective-permute-start.8 = (bf16[200,1600]{1,0:T(8,128)(2,1)}, bf16[200,1600]{1,0:T(8,128)(2,1)}, u32[]{:S(2)}, u32[]{:S(2)}) collective-permute-start(bf16[200,1600]{1,0:T(8,128)(2,1)} %collective-permute-done.5.refs_3_), channel_id=1, source_target_pairs={{0,4},{1,29},{4,8},{5,1},{8,12},{9,5},{12,16},{13,9},{16,20},{17,1... | collective-permute-start | bytes 1920008 | tf_op jit(solution)/shard_map/ppermute | solution.py:131
  52.2 3.8 %collective-permute-done.1.refs_6_ = bf16[200,1600]{1,0:T(8,128)(2,1)} collective-permute-done((bf16[200,1600]{1,0:T(8,128)(2,1)}, bf16[200,1600]{1,0:T(8,128)(2,1)}, u32[]{:S(2)}, u32[]{:S(2)}) %collective-permute-start.1) | collective-permute-done | bytes 640032 | tf_op jit(solution)/shard_map/ppermute | solution.py:131
  56.1 3.3 %collective-permute-start.2 = (bf16[200,1600]{1,0:T(8,128)(2,1)}, bf16[200,1600]{1,0:T(8,128)(2,1)S(1)}, u32[]{:S(2)}, u32[]{:S(2)}) collective-permute-start(bf16[200,1600]{1,0:T(8,128)(2,1)} %collective-permute-done.1.refs_6_), channel_id=1, source_target_pairs={{0,4},{1,29},{4,8},{5,1},{8,12},{9,5},{12,16},{13,9},{16,20},{17,1... | collective-permute-start | bytes 1920008 | tf_op jit(solution)/shard_map/ppermute | solution.py:131
  59.4 0.5 collective-permute-start.10
  59.9 3.3 %collective-permute-done.8.refs_7_ = bf16[200,1600]{1,0:T(8,128)(2,1)} collective-permute-done((bf16[200,1600]{1,0:T(8,128)(2,1)}, bf16[200,1600]{1,0:T(8,128)(2,1)}, u32[]{:S(2)}, u32[]{:S(2)}) %collective-permute-start.8) | collective-permute-done | bytes 640032 | tf_op jit(solution)/shard_map/ppermute | solution.py:131
  63.2 3.1 %collective-permute-start.12 = (bf16[200,1600]{1,0:T(8,128)(2,1)}, bf16[200,1600]{1,0:T(8,128)(2,1)}, u32[]{:S(2)}, u32[]{:S(2)}) collective-permute-start(bf16[200,1600]{1,0:T(8,128)(2,1)} %collective-permute-done.8.refs_7_), channel_id=1, source_target_pairs={{0,4},{1,29},{4,8},{5,1},{8,12},{9,5},{12,16},{13,9},{16,20},{17,1... | collective-permute-start | bytes 1920008 | tf_op jit(solution)/shard_map/ppermute | solution.py:131
  66.3 4.0 %collective-permute-done.2.refs_0_ = bf16[200,1600]{1,0:T(8,128)(2,1)S(1)} collective-permute-done((bf16[200,1600]{1,0:T(8,128)(2,1)}, bf16[200,1600]{1,0:T(8,128)(2,1)S(1)}, u32[]{:S(2)}, u32[]{:S(2)}) %collective-permute-start.2) | collective-permute-done | bytes 640032 | tf_op jit(solution)/shard_map/ppermute | solution.py:131
  70.3 1.6 %collective-permute-start.9 = (bf16[200,1600]{1,0:T(8,128)(2,1)}, bf16[200,1600]{1,0:T(8,128)(2,1)}, u32[]{:S(2)}, u32[]{:S(2)}) collective-permute-start(bf16[200,1600]{1,0:T(8,128)(2,1)} %collective-permute-done.8.refs_7_), channel_id=1, source_target_pairs={{0,1},{1,0},{2,3},{3,2},{4,5},{5,4},{6,7},{7,6},{8,9},{9,8},{10,11... | collective-permute-start | bytes 1920008 | tf_op jit(solution)/shard_map/ppermute | solution.py:104
  72.0 2.0 %collective-permute-start.3 = (bf16[200,1600]{1,0:T(8,128)(2,1)S(1)}, bf16[200,1600]{1,0:T(8,128)(2,1)}, u32[]{:S(2)}, u32[]{:S(2)}) collective-permute-start(bf16[200,1600]{1,0:T(8,128)(2,1)S(1)} %collective-permute-done.2.refs_0_), channel_id=1, source_target_pairs={{0,4},{1,29},{4,8},{5,1},{8,12},{9,5},{12,16},{13,9},{16,20},{17,1... | collective-permute-start | bytes 1920008 | tf_op jit(solution)/shard_map/ppermute | solution.py:131
  74.1 4.1 %copy.16.a_ref = bf16[800,1600]{1,0:T(8,128)(2,1)S(1)} copy(bf16[800,1600]{0,1:T(8,128)(2,1)} %bitcast.35) | data formatting | bytes 5120000 | tf_op jit(solution)/shard_map/optimization_barrier | solution.py:143
  78.5 0.7 collective-permute-start.13
  79.2 14.9 %shard_map.38.refs_5_ = f32[128,256]{1,0:T(8,128)S(1)} custom-call(s32[5]{0:T(128)S(1)} %stack.36.z_ref, bf16[800,1600]{1,0:T(8,128)(2,1)S(1)} %copy.16.a_ref, bf16[200,1600]{1,0:T(8,128)(2,1)} %copy-done.4, bf16[200,1600]{1,0:T(8,128)(2,1)} %collective-permute-done.4.refs_1_, bf16[200,1600]{1,0:T(8,128)(2,1)} %collective-permute-done.refs_2_, ...), custom_call_target="tpu_custom_call" | custom-call | flops 6553600000 | bytes 40000000 | tf_op jit(solution)/shard_map/pallas_call | solution.py:81
  94.1 0.3 collective-permute-start.11
  94.6 6.9 %shard_map.39.refs_3_ = f32[128,256]{1,0:T(8,128)S(1)} custom-call(s32[2]{0:T(128)S(1)} %pad_add_fusion.z_ref, bf16[800,1600]{1,0:T(8,128)(2,1)S(1)} %copy.16.a_ref, bf16[200,1600]{1,0:T(8,128)(2,1)} %copy-done.3, bf16[200,1600]{1,0:T(8,128)(2,1)} %collective-permute-done.12.refs_1_, bf16[200,1600]{1,0:T(8,128)(2,1)} %collective-permute-done.13.refs_2_, ...), custom_call_target="tpu_custom_call" | custom-call | flops 2621440000 | bytes 16000000 | tf_op jit(solution)/shard_map/pallas_call | solution.py:81
  101.5 3.9 %shard_map.40 = f32[128,256]{1,0:T(8,128)S(1)} custom-call(s32[1]{0:T(128)} %bitcast.z_ref, bf16[800,1600]{1,0:T(8,128)(2,1)S(1)} %copy.16.a_ref, bf16[200,1600]{1,0:T(8,128)(2,1)} %collective-permute-done.3.refs_0_, bf16[200,1600]{1,0:T(8,128)(2,1)} %collective-permute-done.11.refs_1_, bf16[8,3200,256]{2,1,0:T(8,128)(2,1)} %bitcast.32, ...), custom_call_target="tpu_custom_call" | custom-call | flops 1310720000 | bytes 8000000 | tf_op jit(solution)/shard_map/pallas_call | solution.py:81
  105.4 17.8 %all_to_all.15 = f32[32,4,256]{2,1,0:T(4,128)S(1)} all-to-all(f32[32,4,256]{2,1,0:T(4,128)S(1)} %bitcast.38), channel_id=1, replica_groups=mesh['y'=4,'xl'=2,'z'=8,'xh'=2,'c'=2] {'z','xh','c'}, dimensions={0} | all-to-all | bytes 262144 | tf_op jit(solution)/shard_map/all_to_all | solution.py:156
  123.3 0.6 reduce_sum.9
  (33 shorter events, 1.1 us)
Async XLA Ops:
  2.2 23.2 %all-to-all-start = ((bf16[32,2,25,200]{3,1,2,0:T(2,128)(2,1)}), bf16[32,2,25,200]{3,1,2,0:T(2,128)(2,1)S(1)}, u32[]{:S(2)}, u32[]{:S(2)}) async-start(bf16[32,2,25,200]{3,1,2,0:T(2,128)(2,1)} %bitcast.1), calls=%async_computation | async-start | bytes 1638400 | tf_op jit(solution)/shard_map/all_to_all | solution.py:121
  10.8 3.9 %copy-start.1 = (bf16[256,25,800]{0,2,1:T(8,128)(2,1)S(1)}, bf16[256,25,800]{0,2,1:T(8,128)(2,1)}, u32[]{:S(2)}) copy-start(bf16[256,25,800]{0,2,1:T(8,128)(2,1)} %param.3) | copy-start | bytes 30720004
  14.7 6.7 %copy-start.5 = (bf16[32,25,200]{2,0,1:T(8,128)(2,1)S(1)}, bf16[32,25,200]{2,0,1:T(8,128)(2,1)}, u32[]{:S(2)}) copy-start(bf16[32,25,200]{2,0,1:T(8,128)(2,1)} %param.4) | copy-start | bytes 960004
  16.7 4.7 %copy-start = (bf16[8,25,128,256]{3,2,1,0:T(8,128)(2,1)}, bf16[8,25,128,256]{3,2,1,0:T(8,128)(2,1)S(1)}, u32[]{:S(2)}) copy-start(bf16[8,25,128,256]{3,2,1,0:T(8,128)(2,1)S(1)} %shard_map.37) | copy-start | bytes 39321604
  28.3 5.8 %copy-start.4 = (bf16[200,1600]{1,0:T(8,128)(2,1)}, bf16[200,1600]{1,0:T(8,128)(2,1)S(1)}, u32[]{:S(2)}) copy-start(bf16[200,1600]{1,0:T(8,128)(2,1)S(1)} %reshape.26.refs_0_) | copy-start | bytes 1920004
  28.3 9.4 %collective-permute-start.4 = (bf16[200,1600]{1,0:T(8,128)(2,1)S(1)}, bf16[200,1600]{1,0:T(8,128)(2,1)}, u32[]{:S(2)}, u32[]{:S(2)}) collective-permute-start(bf16[200,1600]{1,0:T(8,128)(2,1)S(1)} %reshape.26.refs_0_), channel_id=1, source_target_pairs={{0,1},{1,0},{2,3},{3,2},{4,5},{5,4},{6,7},{7,6},{8,9},{9,8},{10,11... | collective-permute-start | bytes 1920008 | tf_op jit(solution)/shard_map/ppermute | solution.py:104
  28.4 13.3 %collective-permute-start = (bf16[200,1600]{1,0:T(8,128)(2,1)S(1)}, bf16[200,1600]{1,0:T(8,128)(2,1)}, u32[]{:S(2)}, u32[]{:S(2)}) collective-permute-start(bf16[200,1600]{1,0:T(8,128)(2,1)S(1)} %reshape.26.refs_0_), channel_id=1, source_target_pairs={{0,4},{1,29},{4,8},{5,1},{8,12},{9,5},{12,16},{13,9},{16,20},{17,1... | collective-permute-start | bytes 1920008 | tf_op jit(solution)/shard_map/ppermute | solution.py:131
  34.0 37.9 %all-to-all-start.1 = ((bf16[8,800,200]{1,2,0:T(8,128)(2,1)}), bf16[8,800,200]{1,2,0:T(8,128)(2,1)S(1)}, u32[]{:S(2)}, u32[]{:S(2)}) async-start(bf16[8,800,200]{1,2,0:T(8,128)(2,1)} %broadcast_in_dim.20), calls=%async_computation.1 | async-start | bytes 5734400 | tf_op jit(solution)/shard_map/all_to_all | solution.py:136
  37.7 11.2 %collective-permute-start.5 = (bf16[200,1600]{1,0:T(8,128)(2,1)}, bf16[200,1600]{1,0:T(8,128)(2,1)}, u32[]{:S(2)}, u32[]{:S(2)}) collective-permute-start(bf16[200,1600]{1,0:T(8,128)(2,1)} %collective-permute-done.4.refs_1_), channel_id=1, source_target_pairs={{0,4},{1,29},{4,8},{5,1},{8,12},{9,5},{12,16},{13,9},{16,20},{17,1... | collective-permute-start | bytes 1920008 | tf_op jit(solution)/shard_map/ppermute | solution.py:131
  41.7 14.4 %collective-permute-start.1 = (bf16[200,1600]{1,0:T(8,128)(2,1)}, bf16[200,1600]{1,0:T(8,128)(2,1)}, u32[]{:S(2)}, u32[]{:S(2)}) collective-permute-start(bf16[200,1600]{1,0:T(8,128)(2,1)} %collective-permute-done.refs_2_), channel_id=1, source_target_pairs={{0,4},{1,29},{4,8},{5,1},{8,12},{9,5},{12,16},{13,9},{16,20},{17,1... | collective-permute-start | bytes 1920008 | tf_op jit(solution)/shard_map/ppermute | solution.py:131
  48.9 14.3 %collective-permute-start.8 = (bf16[200,1600]{1,0:T(8,128)(2,1)}, bf16[200,1600]{1,0:T(8,128)(2,1)}, u32[]{:S(2)}, u32[]{:S(2)}) collective-permute-start(bf16[200,1600]{1,0:T(8,128)(2,1)} %collective-permute-done.5.refs_3_), channel_id=1, source_target_pairs={{0,4},{1,29},{4,8},{5,1},{8,12},{9,5},{12,16},{13,9},{16,20},{17,1... | collective-permute-start | bytes 1920008 | tf_op jit(solution)/shard_map/ppermute | solution.py:131
  56.1 14.3 %collective-permute-start.2 = (bf16[200,1600]{1,0:T(8,128)(2,1)}, bf16[200,1600]{1,0:T(8,128)(2,1)S(1)}, u32[]{:S(2)}, u32[]{:S(2)}) collective-permute-start(bf16[200,1600]{1,0:T(8,128)(2,1)} %collective-permute-done.1.refs_6_), channel_id=1, source_target_pairs={{0,4},{1,29},{4,8},{5,1},{8,12},{9,5},{12,16},{13,9},{16,20},{17,1... | collective-permute-start | bytes 1920008 | tf_op jit(solution)/shard_map/ppermute | solution.py:131
  59.4 12.6 %collective-permute-start.7 = (bf16[200,1600]{1,0:T(8,128)(2,1)}, bf16[200,1600]{1,0:T(8,128)(2,1)}, u32[]{:S(2)}, u32[]{:S(2)}) collective-permute-start(bf16[200,1600]{1,0:T(8,128)(2,1)} %collective-permute-done.refs_2_), channel_id=1, source_target_pairs={{0,1},{1,0},{2,3},{3,2},{4,5},{5,4},{6,7},{7,6},{8,9},{9,8},{10,11... | collective-permute-start | bytes 1920008 | tf_op jit(solution)/shard_map/ppermute | solution.py:104
  59.4 18.9 %collective-permute-start.10 = (bf16[200,1600]{1,0:T(8,128)(2,1)}, bf16[200,1600]{1,0:T(8,128)(2,1)}, u32[]{:S(2)}, u32[]{:S(2)}) collective-permute-start(bf16[200,1600]{1,0:T(8,128)(2,1)} %collective-permute-done.1.refs_6_), channel_id=1, source_target_pairs={{0,1},{1,0},{2,3},{3,2},{4,5},{5,4},{6,7},{7,6},{8,9},{9,8},{10,11... | collective-permute-start | bytes 1920008 | tf_op jit(solution)/shard_map/ppermute | solution.py:104
  63.2 15.3 %collective-permute-start.12 = (bf16[200,1600]{1,0:T(8,128)(2,1)}, bf16[200,1600]{1,0:T(8,128)(2,1)}, u32[]{:S(2)}, u32[]{:S(2)}) collective-permute-start(bf16[200,1600]{1,0:T(8,128)(2,1)} %collective-permute-done.8.refs_7_), channel_id=1, source_target_pairs={{0,4},{1,29},{4,8},{5,1},{8,12},{9,5},{12,16},{13,9},{16,20},{17,1... | collective-permute-start | bytes 1920008 | tf_op jit(solution)/shard_map/ppermute | solution.py:131
  66.3 12.9 %collective-permute-start.6 = (bf16[200,1600]{1,0:T(8,128)(2,1)}, bf16[200,1600]{1,0:T(8,128)(2,1)}, u32[]{:S(2)}, u32[]{:S(2)}) collective-permute-start(bf16[200,1600]{1,0:T(8,128)(2,1)} %collective-permute-done.5.refs_3_), channel_id=1, source_target_pairs={{0,1},{1,0},{2,3},{3,2},{4,5},{5,4},{6,7},{7,6},{8,9},{9,8},{10,11... | collective-permute-start | bytes 1920008 | tf_op jit(solution)/shard_map/ppermute | solution.py:104
  70.3 23.8 %copy-start.3 = (bf16[200,1600]{1,0:T(8,128)(2,1)}, bf16[200,1600]{1,0:T(8,128)(2,1)S(1)}, u32[]{:S(2)}) copy-start(bf16[200,1600]{1,0:T(8,128)(2,1)S(1)} %collective-permute-done.2.refs_0_) | copy-start | bytes 1920004
  70.3 8.9 %collective-permute-start.9 = (bf16[200,1600]{1,0:T(8,128)(2,1)}, bf16[200,1600]{1,0:T(8,128)(2,1)}, u32[]{:S(2)}, u32[]{:S(2)}) collective-permute-start(bf16[200,1600]{1,0:T(8,128)(2,1)} %collective-permute-done.8.refs_7_), channel_id=1, source_target_pairs={{0,1},{1,0},{2,3},{3,2},{4,5},{5,4},{6,7},{7,6},{8,9},{9,8},{10,11... | collective-permute-start | bytes 1920008 | tf_op jit(solution)/shard_map/ppermute | solution.py:104
  71.9 2.0 %copy-start.2 = (bf16[8,800,200]{1,2,0:T(8,128)(2,1)}, bf16[8,800,200]{1,2,0:T(8,128)(2,1)S(1)}, u32[]{:S(2)}) copy-start(bf16[8,800,200]{1,2,0:T(8,128)(2,1)S(1)} %all-to-all-done.1) | copy-start | bytes 7680004
  72.0 22.1 %collective-permute-start.3 = (bf16[200,1600]{1,0:T(8,128)(2,1)S(1)}, bf16[200,1600]{1,0:T(8,128)(2,1)}, u32[]{:S(2)}, u32[]{:S(2)}) collective-permute-start(bf16[200,1600]{1,0:T(8,128)(2,1)S(1)} %collective-permute-done.2.refs_0_), channel_id=1, source_target_pairs={{0,4},{1,29},{4,8},{5,1},{8,12},{9,5},{12,16},{13,9},{16,20},{17,1... | collective-permute-start | bytes 1920008 | tf_op jit(solution)/shard_map/ppermute | solution.py:131
  78.2 16.3 %collective-permute-start.14 = (bf16[200,1600]{1,0:T(8,128)(2,1)S(1)}, bf16[200,1600]{1,0:T(8,128)(2,1)}, u32[]{:S(2)}, u32[]{:S(2)}) collective-permute-start(bf16[200,1600]{1,0:T(8,128)(2,1)S(1)} %collective-permute-done.2.refs_0_), channel_id=1, source_target_pairs={{0,1},{1,0},{2,3},{3,2},{4,5},{5,4},{6,7},{7,6},{8,9},{9,8},{10,11... | collective-permute-start | bytes 1920008 | tf_op jit(solution)/shard_map/ppermute | solution.py:104
  78.5 16.0 %collective-permute-start.13 = (bf16[200,1600]{1,0:T(8,128)(2,1)}, bf16[200,1600]{1,0:T(8,128)(2,1)}, u32[]{:S(2)}, u32[]{:S(2)}) collective-permute-start(bf16[200,1600]{1,0:T(8,128)(2,1)} %collective-permute-done.12.refs_1_), channel_id=1, source_target_pairs={{0,1},{1,0},{2,3},{3,2},{4,5},{5,4},{6,7},{7,6},{8,9},{9,8},{10,11... | collective-permute-start | bytes 1920008 | tf_op jit(solution)/shard_map/ppermute | solution.py:104
  94.1 7.3 %collective-permute-start.11 = (bf16[200,1600]{1,0:T(8,128)(2,1)}, bf16[200,1600]{1,0:T(8,128)(2,1)}, u32[]{:S(2)}, u32[]{:S(2)}) collective-permute-start(bf16[200,1600]{1,0:T(8,128)(2,1)} %collective-permute-done.3.refs_0_), channel_id=1, source_target_pairs={{0,1},{1,0},{2,3},{3,2},{4,5},{5,4},{6,7},{7,6},{8,9},{9,8},{10,11... | collective-permute-start | bytes 1920008 | tf_op jit(solution)/shard_map/ppermute | solution.py:104

commit v3 on v2

--- a/solution.py
+++ b/solution.py
@@ -120,9 +120,9 @@
     send = send.reshape((32,) + halves.shape[1:])
     plane = lax.all_to_all(send, ("y", "xl", "xh", "c"), 0, 0)
 
-    amps = spread(amplitudes.transpose(1, 2, 0), zd)
     a_in = chol_a.transpose(1, 0, 2).reshape(nc * na, npl)
     a_send = jnp.broadcast_to(a_in[None], (8,) + a_in.shape)
+    amps = spread(after(amplitudes.transpose(1, 2, 0), a_send), zd)
     plane, amps, a_send = lax.optimization_barrier((plane, amps, a_send))
     plane = plane.reshape(8, 2, 2, nb // 2, nd, npl)
     own = plane.transpose(3, 1, 2, 4, 0, 5).reshape(nb // 2 * zd, 8 * npl)

time: 124 us -> 123 us (level)
  waiting for transfers between devices: 22 us -> 20.2 us
    all_to_all x1, waiting for transfers between devices: 3.83 us -> 2.06 us  [per_device(): plane = lax.all_to_all(send, ('y', 'xl', 'xh', 'c'), 0, 0)]
  transfers between devices with their start and end apart: 17 -> 17, of which waited for: 6 -> 6; matrix products, arithmetic and copies ran while one was open for 4% -> 5% of each run, Pallas kernels for 19% -> 19%
where the time goes in v3:
time: 123 us; the launch traced here: 122 us
  starting transfers between devices  37.3 us (30%)
  Pallas kernels  27.5 us (22%)
  waiting for transfers between devices  20.2 us (16%)
  local copies, waits for them, and re-layouts  18.3 us (15%)
  blocking collectives  17.9 us (15%)
    pallas_call x3, Pallas kernels, contract(): pl.pallas_call(kernel, grid_spec=pltpu.PrefetchScalarGridSpec(num_scalar_...  25.6 us
    ppermute x7, starting transfers between devices, per_device(): hop = lambda x: lax.ppermute(x, ('z', 'c'), away)  21.4 us
    ppermute x7, waiting for transfers between devices, per_device(): hop = lambda x: lax.ppermute(x, ('z', 'c'), away)  18.2 us
    all_to_all x1, blocking collectives, per_device(): parts = lax.all_to_all(res, ('z', 'xh', 'c'), 0, 0)  17.9 us
    unnamed x12, local copies, waits for them, and re-layouts  8.64 us
    all_to_all x1, starting transfers between devices, per_device(): plane = lax.all_to_all(send, ('y', 'xl', 'xh', 'c'), 0, 0)  8.59 us
    optimization_barrier x1, local copies, waits for them, and re-layouts, per_device(): m3, a = lax.optimization_barrier((m3, a))  4.13 us
    ppermute x8, starting transfers between devices, swap(): return lax.ppermute(x, 'c', [(0, 1), (1, 0)])  3.71 us
  transfers between devices with their start and end apart: 17, of which 6 were waited for; matrix products, arithmetic and copies ran while one was open for 5% of the time, Pallas kernels for 19%

profile of v3, /device:TPU:1, one launch (start us, length us, event | category | flops | bytes accessed | tf_op | source)
XLA Modules:
  0.0 122.2 jit_solution(8023192378445486861)
XLA Ops:
  0.0 0.9 broadcast_in_dim.17
  1.0 1.3 %broadcast_in_dim.18 = bf16[16,2,2,25,200]{4,2,3,1,0:T(2,128)(2,1)} broadcast(bf16[2,2,25,200]{3,1,2,0:T(2,128)(2,1)S(1)} %copy.11), dimensions={1,2,3,4} | broadcast | bytes 680000 | tf_op jit(solution)/shard_map/broadcast_in_dim | solution.py:119
  2.3 8.6 %all-to-all-start = ((bf16[32,2,25,200]{3,1,2,0:T(2,128)(2,1)}), bf16[32,2,25,200]{3,1,2,0:T(2,128)(2,1)S(1)}, u32[]{:S(2)}, u32[]{:S(2)}) async-start(bf16[32,2,25,200]{3,1,2,0:T(2,128)(2,1)} %bitcast.1), calls=%async_computation | async-start | bytes 1638400 | tf_op jit(solution)/shard_map/all_to_all | solution.py:121
  11.1 1.8 %broadcast_in_dim.20 = bf16[8,800,200]{1,2,0:T(8,128)(2,1)} broadcast(bf16[800,200]{0,1:T(8,128)(2,1)S(1)} %copy.12), dimensions={1,2} | broadcast | bytes 2880000 | tf_op jit(solution)/shard_map/broadcast_in_dim | solution.py:124
  12.9 3.9 %copy-done.1 = bf16[256,25,800]{0,2,1:T(8,128)(2,1)S(1)} copy-done((bf16[256,25,800]{0,2,1:T(8,128)(2,1)S(1)}, bf16[256,25,800]{0,2,1:T(8,128)(2,1)}, u32[]{:S(2)}) %copy-start.1) | copy-done | bytes 10240024
  16.8 1.9 %shard_map.37 = bf16[8,25,128,256]{3,2,1,0:T(8,128)(2,1)S(1)} custom-call(bf16[25,800,256]{2,1,0:T(8,128)(2,1)S(1)} %bitcast.33), custom_call_target="tpu_custom_call" | custom-call | bytes 30000000 | tf_op jit(solution)/shard_map/pallas_call | solution.py:23
  18.7 4.7 %copy-done = bf16[8,25,128,256]{3,2,1,0:T(8,128)(2,1)} copy-done((bf16[8,25,128,256]{3,2,1,0:T(8,128)(2,1)}, bf16[8,25,128,256]{3,2,1,0:T(8,128)(2,1)S(1)}, u32[]{:S(2)}) %copy-start) | copy-done | bytes 13107224
  23.4 2.1 %all-to-all-done = bf16[32,2,25,200]{3,1,2,0:T(2,128)(2,1)S(1)} async-done(((bf16[32,2,25,200]{3,1,2,0:T(2,128)(2,1)}), bf16[32,2,25,200]{3,1,2,0:T(2,128)(2,1)S(1)}, u32[]{:S(2)}, u32[]{:S(2)}) %all-to-all-start) | async-done | bytes 640032 | tf_op jit(solution)/shard_map/all_to_all | solution.py:121
  25.6 0.9 reshape.26.refs_0_
  26.7 5.7 %collective-permute-start = (bf16[200,1600]{1,0:T(8,128)(2,1)S(1)}, bf16[200,1600]{1,0:T(8,128)(2,1)}, u32[]{:S(2)}, u32[]{:S(2)}) collective-permute-start(bf16[200,1600]{1,0:T(8,128)(2,1)S(1)} %reshape.26.refs_0_), channel_id=1, source_target_pairs={{0,4},{1,29},{4,8},{5,1},{8,12},{9,5},{12,16},{13,9},{16,20},{17,1... | collective-permute-start | bytes 1920008 | tf_op jit(solution)/shard_map/ppermute | solution.py:131
  32.3 3.6 %all-to-all-start.1 = ((bf16[8,800,200]{1,2,0:T(8,128)(2,1)}), bf16[8,800,200]{1,2,0:T(8,128)(2,1)S(1)}, u32[]{:S(2)}, u32[]{:S(2)}) async-start(bf16[8,800,200]{1,2,0:T(8,128)(2,1)} %broadcast_in_dim.20), calls=%async_computation.1 | async-start | bytes 5734400 | tf_op jit(solution)/shard_map/all_to_all | solution.py:136
  36.0 0.8 collective-permute-start.5
  36.8 3.2 %collective-permute-done.refs_2_ = bf16[200,1600]{1,0:T(8,128)(2,1)} collective-permute-done((bf16[200,1600]{1,0:T(8,128)(2,1)S(1)}, bf16[200,1600]{1,0:T(8,128)(2,1)}, u32[]{:S(2)}, u32[]{:S(2)}) %collective-permute-start) | collective-permute-done | bytes 640032 | tf_op jit(solution)/shard_map/ppermute | solution.py:131
  40.0 3.4 %collective-permute-start.1 = (bf16[200,1600]{1,0:T(8,128)(2,1)}, bf16[200,1600]{1,0:T(8,128)(2,1)}, u32[]{:S(2)}, u32[]{:S(2)}) collective-permute-start(bf16[200,1600]{1,0:T(8,128)(2,1)} %collective-permute-done.refs_2_), channel_id=1, source_target_pairs={{0,4},{1,29},{4,8},{5,1},{8,12},{9,5},{12,16},{13,9},{16,20},{17,1... | collective-permute-start | bytes 1920008 | tf_op jit(solution)/shard_map/ppermute | solution.py:131
  43.4 3.8 %collective-permute-done.5.refs_3_ = bf16[200,1600]{1,0:T(8,128)(2,1)} collective-permute-done((bf16[200,1600]{1,0:T(8,128)(2,1)}, bf16[200,1600]{1,0:T(8,128)(2,1)}, u32[]{:S(2)}, u32[]{:S(2)}) %collective-permute-start.5) | collective-permute-done | bytes 640032 | tf_op jit(solution)/shard_map/ppermute | solution.py:131
  47.2 3.3 %collective-permute-start.8 = (bf16[200,1600]{1,0:T(8,128)(2,1)}, bf16[200,1600]{1,0:T(8,128)(2,1)}, u32[]{:S(2)}, u32[]{:S(2)}) collective-permute-start(bf16[200,1600]{1,0:T(8,128)(2,1)} %collective-permute-done.5.refs_3_), channel_id=1, source_target_pairs={{0,4},{1,29},{4,8},{5,1},{8,12},{9,5},{12,16},{13,9},{16,20},{17,1... | collective-permute-start | bytes 1920008 | tf_op jit(solution)/shard_map/ppermute | solution.py:131
  50.5 3.8 %collective-permute-done.1.refs_6_ = bf16[200,1600]{1,0:T(8,128)(2,1)} collective-permute-done((bf16[200,1600]{1,0:T(8,128)(2,1)}, bf16[200,1600]{1,0:T(8,128)(2,1)}, u32[]{:S(2)}, u32[]{:S(2)}) %collective-permute-start.1) | collective-permute-done | bytes 640032 | tf_op jit(solution)/shard_map/ppermute | solution.py:131
  54.3 3.3 %collective-permute-start.2 = (bf16[200,1600]{1,0:T(8,128)(2,1)}, bf16[200,1600]{1,0:T(8,128)(2,1)S(1)}, u32[]{:S(2)}, u32[]{:S(2)}) collective-permute-start(bf16[200,1600]{1,0:T(8,128)(2,1)} %collective-permute-done.1.refs_6_), channel_id=1, source_target_pairs={{0,4},{1,29},{4,8},{5,1},{8,12},{9,5},{12,16},{13,9},{16,20},{17,1... | collective-permute-start | bytes 1920008 | tf_op jit(solution)/shard_map/ppermute | solution.py:131
  57.6 0.5 collective-permute-start.10
  58.1 3.3 %collective-permute-done.8.refs_7_ = bf16[200,1600]{1,0:T(8,128)(2,1)} collective-permute-done((bf16[200,1600]{1,0:T(8,128)(2,1)}, bf16[200,1600]{1,0:T(8,128)(2,1)}, u32[]{:S(2)}, u32[]{:S(2)}) %collective-permute-start.8) | collective-permute-done | bytes 640032 | tf_op jit(solution)/shard_map/ppermute | solution.py:131
  61.5 3.1 %collective-permute-start.12 = (bf16[200,1600]{1,0:T(8,128)(2,1)}, bf16[200,1600]{1,0:T(8,128)(2,1)}, u32[]{:S(2)}, u32[]{:S(2)}) collective-permute-start(bf16[200,1600]{1,0:T(8,128)(2,1)} %collective-permute-done.8.refs_7_), channel_id=1, source_target_pairs={{0,4},{1,29},{4,8},{5,1},{8,12},{9,5},{12,16},{13,9},{16,20},{17,1... | collective-permute-start | bytes 1920008 | tf_op jit(solution)/shard_map/ppermute | solution.py:131
  64.6 4.0 %collective-permute-done.2.refs_0_ = bf16[200,1600]{1,0:T(8,128)(2,1)S(1)} collective-permute-done((bf16[200,1600]{1,0:T(8,128)(2,1)}, bf16[200,1600]{1,0:T(8,128)(2,1)S(1)}, u32[]{:S(2)}, u32[]{:S(2)}) %collective-permute-start.2) | collective-permute-done | bytes 640032 | tf_op jit(solution)/shard_map/ppermute | solution.py:131
  68.6 1.6 %collective-permute-start.9 = (bf16[200,1600]{1,0:T(8,128)(2,1)}, bf16[200,1600]{1,0:T(8,128)(2,1)}, u32[]{:S(2)}, u32[]{:S(2)}) collective-permute-start(bf16[200,1600]{1,0:T(8,128)(2,1)} %collective-permute-done.8.refs_7_), channel_id=1, source_target_pairs={{0,1},{1,0},{2,3},{3,2},{4,5},{5,4},{6,7},{7,6},{8,9},{9,8},{10,11... | collective-permute-start | bytes 1920008 | tf_op jit(solution)/shard_map/ppermute | solution.py:104
  70.2 1.8 %collective-permute-start.3 = (bf16[200,1600]{1,0:T(8,128)(2,1)S(1)}, bf16[200,1600]{1,0:T(8,128)(2,1)}, u32[]{:S(2)}, u32[]{:S(2)}) collective-permute-start(bf16[200,1600]{1,0:T(8,128)(2,1)S(1)} %collective-permute-done.2.refs_0_), channel_id=1, source_target_pairs={{0,4},{1,29},{4,8},{5,1},{8,12},{9,5},{12,16},{13,9},{16,20},{17,1... | collective-permute-start | bytes 1920008 | tf_op jit(solution)/shard_map/ppermute | solution.py:131
  72.1 4.1 %copy.16.a_ref = bf16[800,1600]{1,0:T(8,128)(2,1)S(1)} copy(bf16[800,1600]{0,1:T(8,128)(2,1)} %bitcast.35) | data formatting | bytes 5120000 | tf_op jit(solution)/shard_map/optimization_barrier | solution.py:143
  76.6 0.9 collective-permute-start.13
  77.5 14.9 %shard_map.38.refs_5_ = f32[128,256]{1,0:T(8,128)S(1)} custom-call(s32[5]{0:T(128)S(1)} %stack.36.z_ref, bf16[800,1600]{1,0:T(8,128)(2,1)S(1)} %copy.16.a_ref, bf16[200,1600]{1,0:T(8,128)(2,1)} %copy-done.4, bf16[200,1600]{1,0:T(8,128)(2,1)} %collective-permute-done.4.refs_1_, bf16[200,1600]{1,0:T(8,128)(2,1)} %collective-permute-done.refs_2_, ...), custom_call_target="tpu_custom_call" | custom-call | flops 6553600000 | bytes 40000000 | tf_op jit(solution)/shard_map/pallas_call | solution.py:81
  92.4 0.3 collective-permute-start.11
  92.8 6.9 %shard_map.39.refs_3_ = f32[128,256]{1,0:T(8,128)S(1)} custom-call(s32[2]{0:T(128)S(1)} %pad_add_fusion.z_ref, bf16[800,1600]{1,0:T(8,128)(2,1)S(1)} %copy.16.a_ref, bf16[200,1600]{1,0:T(8,128)(2,1)} %copy-done.3, bf16[200,1600]{1,0:T(8,128)(2,1)} %collective-permute-done.12.refs_1_, bf16[200,1600]{1,0:T(8,128)(2,1)} %collective-permute-done.13.refs_2_, ...), custom_call_target="tpu_custom_call" | custom-call | flops 2621440000 | bytes 16000000 | tf_op jit(solution)/shard_map/pallas_call | solution.py:81
  99.7 3.9 %shard_map.40 = f32[128,256]{1,0:T(8,128)S(1)} custom-call(s32[1]{0:T(128)} %bitcast.z_ref, bf16[800,1600]{1,0:T(8,128)(2,1)S(1)} %copy.16.a_ref, bf16[200,1600]{1,0:T(8,128)(2,1)} %collective-permute-done.3.refs_0_, bf16[200,1600]{1,0:T(8,128)(2,1)} %collective-permute-done.11.refs_1_, bf16[8,3200,256]{2,1,0:T(8,128)(2,1)} %bitcast.32, ...), custom_call_target="tpu_custom_call" | custom-call | flops 1310720000 | bytes 8000000 | tf_op jit(solution)/shard_map/pallas_call | solution.py:81
  103.7 17.9 %all_to_all.15 = f32[32,4,256]{2,1,0:T(4,128)S(1)} all-to-all(f32[32,4,256]{2,1,0:T(4,128)S(1)} %bitcast.38), channel_id=1, replica_groups=mesh['y'=4,'xl'=2,'z'=8,'xh'=2,'c'=2] {'z','xh','c'}, dimensions={0} | all-to-all | bytes 262144 | tf_op jit(solution)/shard_map/all_to_all | solution.py:156
  121.6 0.6 reduce_sum.9
  (33 shorter events, 1.1 us)
Async XLA Ops:
  0.0 10.9 %copy-start.5 = (bf16[32,25,200]{2,0,1:T(8,128)(2,1)S(1)}, bf16[32,25,200]{2,0,1:T(8,128)(2,1)}, u32[]{:S(2)}) copy-start(bf16[32,25,200]{2,0,1:T(8,128)(2,1)} %param.4) | copy-start | bytes 960004
  2.3 23.2 %all-to-all-start = ((bf16[32,2,25,200]{3,1,2,0:T(2,128)(2,1)}), bf16[32,2,25,200]{3,1,2,0:T(2,128)(2,1)S(1)}, u32[]{:S(2)}, u32[]{:S(2)}) async-start(bf16[32,2,25,200]{3,1,2,0:T(2,128)(2,1)} %bitcast.1), calls=%async_computation | async-start | bytes 1638400 | tf_op jit(solution)/shard_map/all_to_all | solution.py:121
  12.9 3.9 %copy-start.1 = (bf16[256,25,800]{0,2,1:T(8,128)(2,1)S(1)}, bf16[256,25,800]{0,2,1:T(8,128)(2,1)}, u32[]{:S(2)}) copy-start(bf16[256,25,800]{0,2,1:T(8,128)(2,1)} %param.3) | copy-start | bytes 30720004
  18.7 4.7 %copy-start = (bf16[8,25,128,256]{3,2,1,0:T(8,128)(2,1)}, bf16[8,25,128,256]{3,2,1,0:T(8,128)(2,1)S(1)}, u32[]{:S(2)}) copy-start(bf16[8,25,128,256]{3,2,1,0:T(8,128)(2,1)S(1)} %shard_map.37) | copy-start | bytes 39321604
  26.6 5.8 %copy-start.4 = (bf16[200,1600]{1,0:T(8,128)(2,1)}, bf16[200,1600]{1,0:T(8,128)(2,1)S(1)}, u32[]{:S(2)}) copy-start(bf16[200,1600]{1,0:T(8,128)(2,1)S(1)} %reshape.26.refs_0_) | copy-start | bytes 1920004
  26.6 9.4 %collective-permute-start.4 = (bf16[200,1600]{1,0:T(8,128)(2,1)S(1)}, bf16[200,1600]{1,0:T(8,128)(2,1)}, u32[]{:S(2)}, u32[]{:S(2)}) collective-permute-start(bf16[200,1600]{1,0:T(8,128)(2,1)S(1)} %reshape.26.refs_0_), channel_id=1, source_target_pairs={{0,1},{1,0},{2,3},{3,2},{4,5},{5,4},{6,7},{7,6},{8,9},{9,8},{10,11... | collective-permute-start | bytes 1920008 | tf_op jit(solution)/shard_map/ppermute | solution.py:104
  26.7 13.3 %collective-permute-start = (bf16[200,1600]{1,0:T(8,128)(2,1)S(1)}, bf16[200,1600]{1,0:T(8,128)(2,1)}, u32[]{:S(2)}, u32[]{:S(2)}) collective-permute-start(bf16[200,1600]{1,0:T(8,128)(2,1)S(1)} %reshape.26.refs_0_), channel_id=1, source_target_pairs={{0,4},{1,29},{4,8},{5,1},{8,12},{9,5},{12,16},{13,9},{16,20},{17,1... | collective-permute-start | bytes 1920008 | tf_op jit(solution)/shard_map/ppermute | solution.py:131
  32.3 37.9 %all-to-all-start.1 = ((bf16[8,800,200]{1,2,0:T(8,128)(2,1)}), bf16[8,800,200]{1,2,0:T(8,128)(2,1)S(1)}, u32[]{:S(2)}, u32[]{:S(2)}) async-start(bf16[8,800,200]{1,2,0:T(8,128)(2,1)} %broadcast_in_dim.20), calls=%async_computation.1 | async-start | bytes 5734400 | tf_op jit(solution)/shard_map/all_to_all | solution.py:136
  36.0 11.2 %collective-permute-start.5 = (bf16[200,1600]{1,0:T(8,128)(2,1)}, bf16[200,1600]{1,0:T(8,128)(2,1)}, u32[]{:S(2)}, u32[]{:S(2)}) collective-permute-start(bf16[200,1600]{1,0:T(8,128)(2,1)} %collective-permute-done.4.refs_1_), channel_id=1, source_target_pairs={{0,4},{1,29},{4,8},{5,1},{8,12},{9,5},{12,16},{13,9},{16,20},{17,1... | collective-permute-start | bytes 1920008 | tf_op jit(solution)/shard_map/ppermute | solution.py:131
  40.0 14.4 %collective-permute-start.1 = (bf16[200,1600]{1,0:T(8,128)(2,1)}, bf16[200,1600]{1,0:T(8,128)(2,1)}, u32[]{:S(2)}, u32[]{:S(2)}) collective-permute-start(bf16[200,1600]{1,0:T(8,128)(2,1)} %collective-permute-done.refs_2_), channel_id=1, source_target_pairs={{0,4},{1,29},{4,8},{5,1},{8,12},{9,5},{12,16},{13,9},{16,20},{17,1... | collective-permute-start | bytes 1920008 | tf_op jit(solution)/shard_map/ppermute | solution.py:131
  47.2 14.3 %collective-permute-start.8 = (bf16[200,1600]{1,0:T(8,128)(2,1)}, bf16[200,1600]{1,0:T(8,128)(2,1)}, u32[]{:S(2)}, u32[]{:S(2)}) collective-permute-start(bf16[200,1600]{1,0:T(8,128)(2,1)} %collective-permute-done.5.refs_3_), channel_id=1, source_target_pairs={{0,4},{1,29},{4,8},{5,1},{8,12},{9,5},{12,16},{13,9},{16,20},{17,1... | collective-permute-start | bytes 1920008 | tf_op jit(solution)/shard_map/ppermute | solution.py:131
  54.3 14.3 %collective-permute-start.2 = (bf16[200,1600]{1,0:T(8,128)(2,1)}, bf16[200,1600]{1,0:T(8,128)(2,1)S(1)}, u32[]{:S(2)}, u32[]{:S(2)}) collective-permute-start(bf16[200,1600]{1,0:T(8,128)(2,1)} %collective-permute-done.1.refs_6_), channel_id=1, source_target_pairs={{0,4},{1,29},{4,8},{5,1},{8,12},{9,5},{12,16},{13,9},{16,20},{17,1... | collective-permute-start | bytes 1920008 | tf_op jit(solution)/shard_map/ppermute | solution.py:131
  57.6 12.6 %collective-permute-start.7 = (bf16[200,1600]{1,0:T(8,128)(2,1)}, bf16[200,1600]{1,0:T(8,128)(2,1)}, u32[]{:S(2)}, u32[]{:S(2)}) collective-permute-start(bf16[200,1600]{1,0:T(8,128)(2,1)} %collective-permute-done.refs_2_), channel_id=1, source_target_pairs={{0,1},{1,0},{2,3},{3,2},{4,5},{5,4},{6,7},{7,6},{8,9},{9,8},{10,11... | collective-permute-start | bytes 1920008 | tf_op jit(solution)/shard_map/ppermute | solution.py:104
  57.6 18.6 %collective-permute-start.10 = (bf16[200,1600]{1,0:T(8,128)(2,1)}, bf16[200,1600]{1,0:T(8,128)(2,1)}, u32[]{:S(2)}, u32[]{:S(2)}) collective-permute-start(bf16[200,1600]{1,0:T(8,128)(2,1)} %collective-permute-done.1.refs_6_), channel_id=1, source_target_pairs={{0,1},{1,0},{2,3},{3,2},{4,5},{5,4},{6,7},{7,6},{8,9},{9,8},{10,11... | collective-permute-start | bytes 1920008 | tf_op jit(solution)/shard_map/ppermute | solution.py:104
  61.5 15.1 %collective-permute-start.12 = (bf16[200,1600]{1,0:T(8,128)(2,1)}, bf16[200,1600]{1,0:T(8,128)(2,1)}, u32[]{:S(2)}, u32[]{:S(2)}) collective-permute-start(bf16[200,1600]{1,0:T(8,128)(2,1)} %collective-permute-done.8.refs_7_), channel_id=1, source_target_pairs={{0,4},{1,29},{4,8},{5,1},{8,12},{9,5},{12,16},{13,9},{16,20},{17,1... | collective-permute-start | bytes 1920008 | tf_op jit(solution)/shard_map/ppermute | solution.py:131
  64.6 12.9 %collective-permute-start.6 = (bf16[200,1600]{1,0:T(8,128)(2,1)}, bf16[200,1600]{1,0:T(8,128)(2,1)}, u32[]{:S(2)}, u32[]{:S(2)}) collective-permute-start(bf16[200,1600]{1,0:T(8,128)(2,1)} %collective-permute-done.5.refs_3_), channel_id=1, source_target_pairs={{0,1},{1,0},{2,3},{3,2},{4,5},{5,4},{6,7},{7,6},{8,9},{9,8},{10,11... | collective-permute-start | bytes 1920008 | tf_op jit(solution)/shard_map/ppermute | solution.py:104
  68.6 23.8 %copy-start.3 = (bf16[200,1600]{1,0:T(8,128)(2,1)}, bf16[200,1600]{1,0:T(8,128)(2,1)S(1)}, u32[]{:S(2)}) copy-start(bf16[200,1600]{1,0:T(8,128)(2,1)S(1)} %collective-permute-done.2.refs_0_) | copy-start | bytes 1920004
  68.6 8.9 %collective-permute-start.9 = (bf16[200,1600]{1,0:T(8,128)(2,1)}, bf16[200,1600]{1,0:T(8,128)(2,1)}, u32[]{:S(2)}, u32[]{:S(2)}) collective-permute-start(bf16[200,1600]{1,0:T(8,128)(2,1)} %collective-permute-done.8.refs_7_), channel_id=1, source_target_pairs={{0,1},{1,0},{2,3},{3,2},{4,5},{5,4},{6,7},{7,6},{8,9},{9,8},{10,11... | collective-permute-start | bytes 1920008 | tf_op jit(solution)/shard_map/ppermute | solution.py:104
  70.2 1.8 %copy-start.2 = (bf16[8,800,200]{1,2,0:T(8,128)(2,1)}, bf16[8,800,200]{1,2,0:T(8,128)(2,1)S(1)}, u32[]{:S(2)}) copy-start(bf16[8,800,200]{1,2,0:T(8,128)(2,1)S(1)} %all-to-all-done.1) | copy-start | bytes 7680004
  70.2 22.1 %collective-permute-start.3 = (bf16[200,1600]{1,0:T(8,128)(2,1)S(1)}, bf16[200,1600]{1,0:T(8,128)(2,1)}, u32[]{:S(2)}, u32[]{:S(2)}) collective-permute-start(bf16[200,1600]{1,0:T(8,128)(2,1)S(1)} %collective-permute-done.2.refs_0_), channel_id=1, source_target_pairs={{0,4},{1,29},{4,8},{5,1},{8,12},{9,5},{12,16},{13,9},{16,20},{17,1... | collective-permute-start | bytes 1920008 | tf_op jit(solution)/shard_map/ppermute | solution.py:131
  76.3 16.5 %collective-permute-start.14 = (bf16[200,1600]{1,0:T(8,128)(2,1)S(1)}, bf16[200,1600]{1,0:T(8,128)(2,1)}, u32[]{:S(2)}, u32[]{:S(2)}) collective-permute-start(bf16[200,1600]{1,0:T(8,128)(2,1)S(1)} %collective-permute-done.2.refs_0_), channel_id=1, source_target_pairs={{0,1},{1,0},{2,3},{3,2},{4,5},{5,4},{6,7},{7,6},{8,9},{9,8},{10,11... | collective-permute-start | bytes 1920008 | tf_op jit(solution)/shard_map/ppermute | solution.py:104
  76.6 16.3 %collective-permute-start.13 = (bf16[200,1600]{1,0:T(8,128)(2,1)}, bf16[200,1600]{1,0:T(8,128)(2,1)}, u32[]{:S(2)}, u32[]{:S(2)}) collective-permute-start(bf16[200,1600]{1,0:T(8,128)(2,1)} %collective-permute-done.12.refs_1_), channel_id=1, source_target_pairs={{0,1},{1,0},{2,3},{3,2},{4,5},{5,4},{6,7},{7,6},{8,9},{9,8},{10,11... | collective-permute-start | bytes 1920008 | tf_op jit(solution)/shard_map/ppermute | solution.py:104
  92.4 7.3 %collective-permute-start.11 = (bf16[200,1600]{1,0:T(8,128)(2,1)}, bf16[200,1600]{1,0:T(8,128)(2,1)}, u32[]{:S(2)}, u32[]{:S(2)}) collective-permute-start(bf16[200,1600]{1,0:T(8,128)(2,1)} %collective-permute-done.3.refs_0_), channel_id=1, source_target_pairs={{0,1},{1,0},{2,3},{3,2},{4,5},{5,4},{6,7},{7,6},{8,9},{9,8},{10,11... | collective-permute-start | bytes 1920008 | tf_op jit(solution)/shard_map/ppermute | solution.py:104

commit v4 on v3

--- a/solution.py
+++ b/solution.py
@@ -93,7 +93,7 @@
             ],
         ),
         out_shape=jax.ShapeDtypeStruct(acc.shape, jnp.float32),
-        compiler_params=pltpu.CompilerParams(vmem_limit_bytes=40 * 1024 * 1024),
+        compiler_params=pltpu.CompilerParams(vmem_limit_bytes=24 * 1024 * 1024),
         cost_estimate=pl.CostEstimate(
             flops=n * 2 * 128 * cols * 1600, bytes_accessed=n * 8_000_000, transcendentals=0
         ),

time: 123 us -> 123 us (level)
  no operation moved by 1% of the time
where the time goes in v4:
time: 123 us; the launch traced here: 122 us
  starting transfers between devices  37.3 us (30%)
  Pallas kernels  27.5 us (22%)
  waiting for transfers between devices  20.2 us (16%)
  local copies, waits for them, and re-layouts  18.3 us (15%)
  blocking collectives  17.9 us (15%)
    pallas_call x3, Pallas kernels, contract(): pl.pallas_call(kernel, grid_spec=pltpu.PrefetchScalarGridSpec(num_scalar_...  25.6 us
    ppermute x7, starting transfers between devices, per_device(): hop = lambda x: lax.ppermute(x, ('z', 'c'), away)  21.4 us
    ppermute x7, waiting for transfers between devices, per_device(): hop = lambda x: lax.ppermute(x, ('z', 'c'), away)  18.2 us
    all_to_all x1, blocking collectives, per_device(): parts = lax.all_to_all(res, ('z', 'xh', 'c'), 0, 0)  17.9 us
    unnamed x12, local copies, waits for them, and re-layouts  8.64 us
    all_to_all x1, starting transfers between devices, per_device(): plane = lax.all_to_all(send, ('y', 'xl', 'xh', 'c'), 0, 0)  8.59 us
    optimization_barrier x1, local copies, waits for them, and re-layouts, per_device(): m3, a = lax.optimization_barrier((m3, a))  4.13 us
    ppermute x8, starting transfers between devices, swap(): return lax.ppermute(x, 'c', [(0, 1), (1, 0)])  3.71 us
  transfers between devices with their start and end apart: 17, of which 6 were waited for; matrix products, arithmetic and copies ran while one was open for 5% of the time, Pallas kernels for 19%

profile of v4, /device:TPU:1, one launch (start us, length us, event | category | flops | bytes accessed | tf_op | source)
XLA Modules:
  0.0 122.2 jit_solution(11582345373357234126)
XLA Ops:
  0.0 0.9 broadcast_in_dim.17
  1.0 1.3 %broadcast_in_dim.18 = bf16[16,2,2,25,200]{4,2,3,1,0:T(2,128)(2,1)} broadcast(bf16[2,2,25,200]{3,1,2,0:T(2,128)(2,1)S(1)} %copy.11), dimensions={1,2,3,4} | broadcast | bytes 680000 | tf_op jit(solution)/shard_map/broadcast_in_dim | solution.py:119
  2.3 8.6 %all-to-all-start = ((bf16[32,2,25,200]{3,1,2,0:T(2,128)(2,1)}), bf16[32,2,25,200]{3,1,2,0:T(2,128)(2,1)S(1)}, u32[]{:S(2)}, u32[]{:S(2)}) async-start(bf16[32,2,25,200]{3,1,2,0:T(2,128)(2,1)} %bitcast.1), calls=%async_computation | async-start | bytes 1638400 | tf_op jit(solution)/shard_map/all_to_all | solution.py:121
  11.1 1.8 %broadcast_in_dim.20 = bf16[8,800,200]{1,2,0:T(8,128)(2,1)} broadcast(bf16[800,200]{0,1:T(8,128)(2,1)S(1)} %copy.12), dimensions={1,2} | broadcast | bytes 2880000 | tf_op jit(solution)/shard_map/broadcast_in_dim | solution.py:124
  12.9 3.9 %copy-done.1 = bf16[256,25,800]{0,2,1:T(8,128)(2,1)S(1)} copy-done((bf16[256,25,800]{0,2,1:T(8,128)(2,1)S(1)}, bf16[256,25,800]{0,2,1:T(8,128)(2,1)}, u32[]{:S(2)}) %copy-start.1) | copy-done | bytes 10240024
  16.8 1.9 %shard_map.37 = bf16[8,25,128,256]{3,2,1,0:T(8,128)(2,1)S(1)} custom-call(bf16[25,800,256]{2,1,0:T(8,128)(2,1)S(1)} %bitcast.33), custom_call_target="tpu_custom_call" | custom-call | bytes 30000000 | tf_op jit(solution)/shard_map/pallas_call | solution.py:23
  18.7 4.7 %copy-done = bf16[8,25,128,256]{3,2,1,0:T(8,128)(2,1)} copy-done((bf16[8,25,128,256]{3,2,1,0:T(8,128)(2,1)}, bf16[8,25,128,256]{3,2,1,0:T(8,128)(2,1)S(1)}, u32[]{:S(2)}) %copy-start) | copy-done | bytes 13107224
  23.4 2.1 %all-to-all-done = bf16[32,2,25,200]{3,1,2,0:T(2,128)(2,1)S(1)} async-done(((bf16[32,2,25,200]{3,1,2,0:T(2,128)(2,1)}), bf16[32,2,25,200]{3,1,2,0:T(2,128)(2,1)S(1)}, u32[]{:S(2)}, u32[]{:S(2)}) %all-to-all-start) | async-done | bytes 640032 | tf_op jit(solution)/shard_map/all_to_all | solution.py:121
  25.6 0.9 reshape.26.refs_0_
  26.7 5.7 %collective-permute-start = (bf16[200,1600]{1,0:T(8,128)(2,1)S(1)}, bf16[200,1600]{1,0:T(8,128)(2,1)}, u32[]{:S(2)}, u32[]{:S(2)}) collective-permute-start(bf16[200,1600]{1,0:T(8,128)(2,1)S(1)} %reshape.26.refs_0_), channel_id=1, source_target_pairs={{0,4},{1,29},{4,8},{5,1},{8,12},{9,5},{12,16},{13,9},{16,20},{17,1... | collective-permute-start | bytes 1920008 | tf_op jit(solution)/shard_map/ppermute | solution.py:131
  32.3 3.6 %all-to-all-start.1 = ((bf16[8,800,200]{1,2,0:T(8,128)(2,1)}), bf16[8,800,200]{1,2,0:T(8,128)(2,1)S(1)}, u32[]{:S(2)}, u32[]{:S(2)}) async-start(bf16[8,800,200]{1,2,0:T(8,128)(2,1)} %broadcast_in_dim.20), calls=%async_computation.1 | async-start | bytes 5734400 | tf_op jit(solution)/shard_map/all_to_all | solution.py:136
  36.0 0.8 collective-permute-start.5
  36.8 3.2 %collective-permute-done.refs_2_ = bf16[200,1600]{1,0:T(8,128)(2,1)} collective-permute-done((bf16[200,1600]{1,0:T(8,128)(2,1)S(1)}, bf16[200,1600]{1,0:T(8,128)(2,1)}, u32[]{:S(2)}, u32[]{:S(2)}) %collective-permute-start) | collective-permute-done | bytes 640032 | tf_op jit(solution)/shard_map/ppermute | solution.py:131
  40.0 3.4 %collective-permute-start.1 = (bf16[200,1600]{1,0:T(8,128)(2,1)}, bf16[200,1600]{1,0:T(8,128)(2,1)}, u32[]{:S(2)}, u32[]{:S(2)}) collective-permute-start(bf16[200,1600]{1,0:T(8,128)(2,1)} %collective-permute-done.refs_2_), channel_id=1, source_target_pairs={{0,4},{1,29},{4,8},{5,1},{8,12},{9,5},{12,16},{13,9},{16,20},{17,1... | collective-permute-start | bytes 1920008 | tf_op jit(solution)/shard_map/ppermute | solution.py:131
  43.4 3.8 %collective-permute-done.5.refs_3_ = bf16[200,1600]{1,0:T(8,128)(2,1)} collective-permute-done((bf16[200,1600]{1,0:T(8,128)(2,1)}, bf16[200,1600]{1,0:T(8,128)(2,1)}, u32[]{:S(2)}, u32[]{:S(2)}) %collective-permute-start.5) | collective-permute-done | bytes 640032 | tf_op jit(solution)/shard_map/ppermute | solution.py:131
  47.2 3.3 %collective-permute-start.8 = (bf16[200,1600]{1,0:T(8,128)(2,1)}, bf16[200,1600]{1,0:T(8,128)(2,1)}, u32[]{:S(2)}, u32[]{:S(2)}) collective-permute-start(bf16[200,1600]{1,0:T(8,128)(2,1)} %collective-permute-done.5.refs_3_), channel_id=1, source_target_pairs={{0,4},{1,29},{4,8},{5,1},{8,12},{9,5},{12,16},{13,9},{16,20},{17,1... | collective-permute-start | bytes 1920008 | tf_op jit(solution)/shard_map/ppermute | solution.py:131
  50.5 3.8 %collective-permute-done.1.refs_6_ = bf16[200,1600]{1,0:T(8,128)(2,1)} collective-permute-done((bf16[200,1600]{1,0:T(8,128)(2,1)}, bf16[200,1600]{1,0:T(8,128)(2,1)}, u32[]{:S(2)}, u32[]{:S(2)}) %collective-permute-start.1) | collective-permute-done | bytes 640032 | tf_op jit(solution)/shard_map/ppermute | solution.py:131
  54.3 3.3 %collective-permute-start.2 = (bf16[200,1600]{1,0:T(8,128)(2,1)}, bf16[200,1600]{1,0:T(8,128)(2,1)S(1)}, u32[]{:S(2)}, u32[]{:S(2)}) collective-permute-start(bf16[200,1600]{1,0:T(8,128)(2,1)} %collective-permute-done.1.refs_6_), channel_id=1, source_target_pairs={{0,4},{1,29},{4,8},{5,1},{8,12},{9,5},{12,16},{13,9},{16,20},{17,1... | collective-permute-start | bytes 1920008 | tf_op jit(solution)/shard_map/ppermute | solution.py:131
  57.6 0.5 collective-permute-start.10
  58.1 3.3 %collective-permute-done.8.refs_7_ = bf16[200,1600]{1,0:T(8,128)(2,1)} collective-permute-done((bf16[200,1600]{1,0:T(8,128)(2,1)}, bf16[200,1600]{1,0:T(8,128)(2,1)}, u32[]{:S(2)}, u32[]{:S(2)}) %collective-permute-start.8) | collective-permute-done | bytes 640032 | tf_op jit(solution)/shard_map/ppermute | solution.py:131
  61.5 3.1 %collective-permute-start.12 = (bf16[200,1600]{1,0:T(8,128)(2,1)}, bf16[200,1600]{1,0:T(8,128)(2,1)}, u32[]{:S(2)}, u32[]{:S(2)}) collective-permute-start(bf16[200,1600]{1,0:T(8,128)(2,1)} %collective-permute-done.8.refs_7_), channel_id=1, source_target_pairs={{0,4},{1,29},{4,8},{5,1},{8,12},{9,5},{12,16},{13,9},{16,20},{17,1... | collective-permute-start | bytes 1920008 | tf_op jit(solution)/shard_map/ppermute | solution.py:131
  64.6 4.0 %collective-permute-done.2.refs_0_ = bf16[200,1600]{1,0:T(8,128)(2,1)S(1)} collective-permute-done((bf16[200,1600]{1,0:T(8,128)(2,1)}, bf16[200,1600]{1,0:T(8,128)(2,1)S(1)}, u32[]{:S(2)}, u32[]{:S(2)}) %collective-permute-start.2) | collective-permute-done | bytes 640032 | tf_op jit(solution)/shard_map/ppermute | solution.py:131
  68.6 1.6 %collective-permute-start.9 = (bf16[200,1600]{1,0:T(8,128)(2,1)}, bf16[200,1600]{1,0:T(8,128)(2,1)}, u32[]{:S(2)}, u32[]{:S(2)}) collective-permute-start(bf16[200,1600]{1,0:T(8,128)(2,1)} %collective-permute-done.8.refs_7_), channel_id=1, source_target_pairs={{0,1},{1,0},{2,3},{3,2},{4,5},{5,4},{6,7},{7,6},{8,9},{9,8},{10,11... | collective-permute-start | bytes 1920008 | tf_op jit(solution)/shard_map/ppermute | solution.py:104
  70.2 1.8 %collective-permute-start.3 = (bf16[200,1600]{1,0:T(8,128)(2,1)S(1)}, bf16[200,1600]{1,0:T(8,128)(2,1)}, u32[]{:S(2)}, u32[]{:S(2)}) collective-permute-start(bf16[200,1600]{1,0:T(8,128)(2,1)S(1)} %collective-permute-done.2.refs_0_), channel_id=1, source_target_pairs={{0,4},{1,29},{4,8},{5,1},{8,12},{9,5},{12,16},{13,9},{16,20},{17,1... | collective-permute-start | bytes 1920008 | tf_op jit(solution)/shard_map/ppermute | solution.py:131
  72.1 4.1 %copy.16.a_ref = bf16[800,1600]{1,0:T(8,128)(2,1)S(1)} copy(bf16[800,1600]{0,1:T(8,128)(2,1)} %bitcast.35) | data formatting | bytes 5120000 | tf_op jit(solution)/shard_map/optimization_barrier | solution.py:143
  76.6 0.9 collective-permute-start.13
  77.5 14.9 %shard_map.38.refs_5_ = f32[128,256]{1,0:T(8,128)S(1)} custom-call(s32[5]{0:T(128)S(1)} %stack.36.z_ref, bf16[800,1600]{1,0:T(8,128)(2,1)S(1)} %copy.16.a_ref, bf16[200,1600]{1,0:T(8,128)(2,1)} %copy-done.4, bf16[200,1600]{1,0:T(8,128)(2,1)} %collective-permute-done.4.refs_1_, bf16[200,1600]{1,0:T(8,128)(2,1)} %collective-permute-done.refs_2_, ...), custom_call_target="tpu_custom_call" | custom-call | flops 6553600000 | bytes 40000000 | tf_op jit(solution)/shard_map/pallas_call | solution.py:81
  92.4 0.3 collective-permute-start.11
  92.8 6.9 %shard_map.39.refs_3_ = f32[128,256]{1,0:T(8,128)S(1)} custom-call(s32[2]{0:T(128)S(1)} %pad_add_fusion.z_ref, bf16[800,1600]{1,0:T(8,128)(2,1)S(1)} %copy.16.a_ref, bf16[200,1600]{1,0:T(8,128)(2,1)} %copy-done.3, bf16[200,1600]{1,0:T(8,128)(2,1)} %collective-permute-done.12.refs_1_, bf16[200,1600]{1,0:T(8,128)(2,1)} %collective-permute-done.13.refs_2_, ...), custom_call_target="tpu_custom_call" | custom-call | flops 2621440000 | bytes 16000000 | tf_op jit(solution)/shard_map/pallas_call | solution.py:81
  99.7 3.9 %shard_map.40 = f32[128,256]{1,0:T(8,128)S(1)} custom-call(s32[1]{0:T(128)} %bitcast.z_ref, bf16[800,1600]{1,0:T(8,128)(2,1)S(1)} %copy.16.a_ref, bf16[200,1600]{1,0:T(8,128)(2,1)} %collective-permute-done.3.refs_0_, bf16[200,1600]{1,0:T(8,128)(2,1)} %collective-permute-done.11.refs_1_, bf16[8,3200,256]{2,1,0:T(8,128)(2,1)} %bitcast.32, ...), custom_call_target="tpu_custom_call" | custom-call | flops 1310720000 | bytes 8000000 | tf_op jit(solution)/shard_map/pallas_call | solution.py:81
  103.7 17.9 %all_to_all.15 = f32[32,4,256]{2,1,0:T(4,128)S(1)} all-to-all(f32[32,4,256]{2,1,0:T(4,128)S(1)} %bitcast.38), channel_id=1, replica_groups=mesh['y'=4,'xl'=2,'z'=8,'xh'=2,'c'=2] {'z','xh','c'}, dimensions={0} | all-to-all | bytes 262144 | tf_op jit(solution)/shard_map/all_to_all | solution.py:156
  121.6 0.6 reduce_sum.9
  (33 shorter events, 1.1 us)
Async XLA Ops:
  0.0 10.9 %copy-start.5 = (bf16[32,25,200]{2,0,1:T(8,128)(2,1)S(1)}, bf16[32,25,200]{2,0,1:T(8,128)(2,1)}, u32[]{:S(2)}) copy-start(bf16[32,25,200]{2,0,1:T(8,128)(2,1)} %param.4) | copy-start | bytes 960004
  2.3 23.2 %all-to-all-start = ((bf16[32,2,25,200]{3,1,2,0:T(2,128)(2,1)}), bf16[32,2,25,200]{3,1,2,0:T(2,128)(2,1)S(1)}, u32[]{:S(2)}, u32[]{:S(2)}) async-start(bf16[32,2,25,200]{3,1,2,0:T(2,128)(2,1)} %bitcast.1), calls=%async_computation | async-start | bytes 1638400 | tf_op jit(solution)/shard_map/all_to_all | solution.py:121
  12.9 3.9 %copy-start.1 = (bf16[256,25,800]{0,2,1:T(8,128)(2,1)S(1)}, bf16[256,25,800]{0,2,1:T(8,128)(2,1)}, u32[]{:S(2)}) copy-start(bf16[256,25,800]{0,2,1:T(8,128)(2,1)} %param.3) | copy-start | bytes 30720004
  18.7 4.7 %copy-start = (bf16[8,25,128,256]{3,2,1,0:T(8,128)(2,1)}, bf16[8,25,128,256]{3,2,1,0:T(8,128)(2,1)S(1)}, u32[]{:S(2)}) copy-start(bf16[8,25,128,256]{3,2,1,0:T(8,128)(2,1)S(1)} %shard_map.37) | copy-start | bytes 39321604
  26.6 5.8 %copy-start.4 = (bf16[200,1600]{1,0:T(8,128)(2,1)}, bf16[200,1600]{1,0:T(8,128)(2,1)S(1)}, u32[]{:S(2)}) copy-start(bf16[200,1600]{1,0:T(8,128)(2,1)S(1)} %reshape.26.refs_0_) | copy-start | bytes 1920004
  26.6 9.4 %collective-permute-start.4 = (bf16[200,1600]{1,0:T(8,128)(2,1)S(1)}, bf16[200,1600]{1,0:T(8,128)(2,1)}, u32[]{:S(2)}, u32[]{:S(2)}) collective-permute-start(bf16[200,1600]{1,0:T(8,128)(2,1)S(1)} %reshape.26.refs_0_), channel_id=1, source_target_pairs={{0,1},{1,0},{2,3},{3,2},{4,5},{5,4},{6,7},{7,6},{8,9},{9,8},{10,11... | collective-permute-start | bytes 1920008 | tf_op jit(solution)/shard_map/ppermute | solution.py:104
  26.7 13.3 %collective-permute-start = (bf16[200,1600]{1,0:T(8,128)(2,1)S(1)}, bf16[200,1600]{1,0:T(8,128)(2,1)}, u32[]{:S(2)}, u32[]{:S(2)}) collective-permute-start(bf16[200,1600]{1,0:T(8,128)(2,1)S(1)} %reshape.26.refs_0_), channel_id=1, source_target_pairs={{0,4},{1,29},{4,8},{5,1},{8,12},{9,5},{12,16},{13,9},{16,20},{17,1... | collective-permute-start | bytes 1920008 | tf_op jit(solution)/shard_map/ppermute | solution.py:131
  32.3 37.9 %all-to-all-start.1 = ((bf16[8,800,200]{1,2,0:T(8,128)(2,1)}), bf16[8,800,200]{1,2,0:T(8,128)(2,1)S(1)}, u32[]{:S(2)}, u32[]{:S(2)}) async-start(bf16[8,800,200]{1,2,0:T(8,128)(2,1)} %broadcast_in_dim.20), calls=%async_computation.1 | async-start | bytes 5734400 | tf_op jit(solution)/shard_map/all_to_all | solution.py:136
  36.0 11.2 %collective-permute-start.5 = (bf16[200,1600]{1,0:T(8,128)(2,1)}, bf16[200,1600]{1,0:T(8,128)(2,1)}, u32[]{:S(2)}, u32[]{:S(2)}) collective-permute-start(bf16[200,1600]{1,0:T(8,128)(2,1)} %collective-permute-done.4.refs_1_), channel_id=1, source_target_pairs={{0,4},{1,29},{4,8},{5,1},{8,12},{9,5},{12,16},{13,9},{16,20},{17,1... | collective-permute-start | bytes 1920008 | tf_op jit(solution)/shard_map/ppermute | solution.py:131
  40.0 14.4 %collective-permute-start.1 = (bf16[200,1600]{1,0:T(8,128)(2,1)}, bf16[200,1600]{1,0:T(8,128)(2,1)}, u32[]{:S(2)}, u32[]{:S(2)}) collective-permute-start(bf16[200,1600]{1,0:T(8,128)(2,1)} %collective-permute-done.refs_2_), channel_id=1, source_target_pairs={{0,4},{1,29},{4,8},{5,1},{8,12},{9,5},{12,16},{13,9},{16,20},{17,1... | collective-permute-start | bytes 1920008 | tf_op jit(solution)/shard_map/ppermute | solution.py:131
  47.2 14.3 %collective-permute-start.8 = (bf16[200,1600]{1,0:T(8,128)(2,1)}, bf16[200,1600]{1,0:T(8,128)(2,1)}, u32[]{:S(2)}, u32[]{:S(2)}) collective-permute-start(bf16[200,1600]{1,0:T(8,128)(2,1)} %collective-permute-done.5.refs_3_), channel_id=1, source_target_pairs={{0,4},{1,29},{4,8},{5,1},{8,12},{9,5},{12,16},{13,9},{16,20},{17,1... | collective-permute-start | bytes 1920008 | tf_op jit(solution)/shard_map/ppermute | solution.py:131
  54.3 14.3 %collective-permute-start.2 = (bf16[200,1600]{1,0:T(8,128)(2,1)}, bf16[200,1600]{1,0:T(8,128)(2,1)S(1)}, u32[]{:S(2)}, u32[]{:S(2)}) collective-permute-start(bf16[200,1600]{1,0:T(8,128)(2,1)} %collective-permute-done.1.refs_6_), channel_id=1, source_target_pairs={{0,4},{1,29},{4,8},{5,1},{8,12},{9,5},{12,16},{13,9},{16,20},{17,1... | collective-permute-start | bytes 1920008 | tf_op jit(solution)/shard_map/ppermute | solution.py:131
  57.6 12.6 %collective-permute-start.7 = (bf16[200,1600]{1,0:T(8,128)(2,1)}, bf16[200,1600]{1,0:T(8,128)(2,1)}, u32[]{:S(2)}, u32[]{:S(2)}) collective-permute-start(bf16[200,1600]{1,0:T(8,128)(2,1)} %collective-permute-done.refs_2_), channel_id=1, source_target_pairs={{0,1},{1,0},{2,3},{3,2},{4,5},{5,4},{6,7},{7,6},{8,9},{9,8},{10,11... | collective-permute-start | bytes 1920008 | tf_op jit(solution)/shard_map/ppermute | solution.py:104
  57.6 18.6 %collective-permute-start.10 = (bf16[200,1600]{1,0:T(8,128)(2,1)}, bf16[200,1600]{1,0:T(8,128)(2,1)}, u32[]{:S(2)}, u32[]{:S(2)}) collective-permute-start(bf16[200,1600]{1,0:T(8,128)(2,1)} %collective-permute-done.1.refs_6_), channel_id=1, source_target_pairs={{0,1},{1,0},{2,3},{3,2},{4,5},{5,4},{6,7},{7,6},{8,9},{9,8},{10,11... | collective-permute-start | bytes 1920008 | tf_op jit(solution)/shard_map/ppermute | solution.py:104
  61.5 15.1 %collective-permute-start.12 = (bf16[200,1600]{1,0:T(8,128)(2,1)}, bf16[200,1600]{1,0:T(8,128)(2,1)}, u32[]{:S(2)}, u32[]{:S(2)}) collective-permute-start(bf16[200,1600]{1,0:T(8,128)(2,1)} %collective-permute-done.8.refs_7_), channel_id=1, source_target_pairs={{0,4},{1,29},{4,8},{5,1},{8,12},{9,5},{12,16},{13,9},{16,20},{17,1... | collective-permute-start | bytes 1920008 | tf_op jit(solution)/shard_map/ppermute | solution.py:131
  64.6 12.9 %collective-permute-start.6 = (bf16[200,1600]{1,0:T(8,128)(2,1)}, bf16[200,1600]{1,0:T(8,128)(2,1)}, u32[]{:S(2)}, u32[]{:S(2)}) collective-permute-start(bf16[200,1600]{1,0:T(8,128)(2,1)} %collective-permute-done.5.refs_3_), channel_id=1, source_target_pairs={{0,1},{1,0},{2,3},{3,2},{4,5},{5,4},{6,7},{7,6},{8,9},{9,8},{10,11... | collective-permute-start | bytes 1920008 | tf_op jit(solution)/shard_map/ppermute | solution.py:104
  68.6 23.8 %copy-start.3 = (bf16[200,1600]{1,0:T(8,128)(2,1)}, bf16[200,1600]{1,0:T(8,128)(2,1)S(1)}, u32[]{:S(2)}) copy-start(bf16[200,1600]{1,0:T(8,128)(2,1)S(1)} %collective-permute-done.2.refs_0_) | copy-start | bytes 1920004
  68.6 8.9 %collective-permute-start.9 = (bf16[200,1600]{1,0:T(8,128)(2,1)}, bf16[200,1600]{1,0:T(8,128)(2,1)}, u32[]{:S(2)}, u32[]{:S(2)}) collective-permute-start(bf16[200,1600]{1,0:T(8,128)(2,1)} %collective-permute-done.8.refs_7_), channel_id=1, source_target_pairs={{0,1},{1,0},{2,3},{3,2},{4,5},{5,4},{6,7},{7,6},{8,9},{9,8},{10,11... | collective-permute-start | bytes 1920008 | tf_op jit(solution)/shard_map/ppermute | solution.py:104
  70.2 1.8 %copy-start.2 = (bf16[8,800,200]{1,2,0:T(8,128)(2,1)}, bf16[8,800,200]{1,2,0:T(8,128)(2,1)S(1)}, u32[]{:S(2)}) copy-start(bf16[8,800,200]{1,2,0:T(8,128)(2,1)S(1)} %all-to-all-done.1) | copy-start | bytes 7680004
  70.2 22.1 %collective-permute-start.3 = (bf16[200,1600]{1,0:T(8,128)(2,1)S(1)}, bf16[200,1600]{1,0:T(8,128)(2,1)}, u32[]{:S(2)}, u32[]{:S(2)}) collective-permute-start(bf16[200,1600]{1,0:T(8,128)(2,1)S(1)} %collective-permute-done.2.refs_0_), channel_id=1, source_target_pairs={{0,4},{1,29},{4,8},{5,1},{8,12},{9,5},{12,16},{13,9},{16,20},{17,1... | collective-permute-start | bytes 1920008 | tf_op jit(solution)/shard_map/ppermute | solution.py:131
  76.3 16.5 %collective-permute-start.14 = (bf16[200,1600]{1,0:T(8,128)(2,1)S(1)}, bf16[200,1600]{1,0:T(8,128)(2,1)}, u32[]{:S(2)}, u32[]{:S(2)}) collective-permute-start(bf16[200,1600]{1,0:T(8,128)(2,1)S(1)} %collective-permute-done.2.refs_0_), channel_id=1, source_target_pairs={{0,1},{1,0},{2,3},{3,2},{4,5},{5,4},{6,7},{7,6},{8,9},{9,8},{10,11... | collective-permute-start | bytes 1920008 | tf_op jit(solution)/shard_map/ppermute | solution.py:104
  76.6 16.3 %collective-permute-start.13 = (bf16[200,1600]{1,0:T(8,128)(2,1)}, bf16[200,1600]{1,0:T(8,128)(2,1)}, u32[]{:S(2)}, u32[]{:S(2)}) collective-permute-start(bf16[200,1600]{1,0:T(8,128)(2,1)} %collective-permute-done.12.refs_1_), channel_id=1, source_target_pairs={{0,1},{1,0},{2,3},{3,2},{4,5},{5,4},{6,7},{7,6},{8,9},{9,8},{10,11... | collective-permute-start | bytes 1920008 | tf_op jit(solution)/shard_map/ppermute | solution.py:104
  92.4 7.3 %collective-permute-start.11 = (bf16[200,1600]{1,0:T(8,128)(2,1)}, bf16[200,1600]{1,0:T(8,128)(2,1)}, u32[]{:S(2)}, u32[]{:S(2)}) collective-permute-start(bf16[200,1600]{1,0:T(8,128)(2,1)} %collective-permute-done.3.refs_0_), channel_id=1, source_target_pairs={{0,1},{1,0},{2,3},{3,2},{4,5},{5,4},{6,7},{7,6},{8,9},{9,8},{10,11... | collective-permute-start | bytes 1920008 | tf_op jit(solution)/shard_map/ppermute | solution.py:104
